TPU v7x, 128 devices: a whole 4x4x4 slice. The times are simulated.
128 devices in a mesh: ta: 4 (over x), sa: 32 (over z, y, core).
Axes of the slice: x: 4, y: 4, z: 4, core: 2. Of those that a mesh axis runs over, the one named last changes fastest.
Arguments:
- start: float32 [8, 3, 32, 32, 32, 128], P('ta', None, 'sa'), parts along dimension 0, may hold values from -10 to 10
- links: float32 [12, 2, 3, 3, 32, 32, 32], P('ta', None, None, None, 'sa'), parts along dimension 0, may hold values from -1 to 1, as said below
- momenta: int32 [7, 3], replicated, may hold values from -2 to 2
- displace: int32 [3], replicated, may hold values from 0 to 2, each once
Outputs:
- basis: float32 [8, 3, 32, 32, 32, 128], P('ta', None, 'sa'), parts along dimension 0
- ritz: float32 [8, 128, 128], P('ta'), parts along dimension 0
- phi: float32 [128, 28, 3, 2, 128], P('sa', 'ta'), parts along dimension 1
There are 4 independent parts, one for each index of `ta`. A program takes and returns all parts, laid end to end along the dimension named above; an argument that names none is the same for every part. Nothing has to cross between parts.
Inputs may be any that keep to these rules, and one draw needn't show every extreme that they name: `links`: each 3 x 3 complex matrix of one direction and site is special unitary. `displace`: names each of the three directions once.
All inputs are finite; a program needn't handle non-finite values.
Results may differ from a plain program's by a relative error of at most 0.0002.
Values sent between devices are 32-bit elements; how exact they have to be, the bound alone decides.
No kernel may reach another device: no remote copies, remote signals or barrier semaphores. Data moves between devices by JAX's collectives and lax.ppermute only.
A program may use at most 576 MiB of HBM per device.

v0:
```python
import math

import jax
import jax.numpy as jnp
from jax import lax
from jax.experimental import pallas as pl
from jax.experimental.pallas import tpu as pltpu
from jax.sharding import PartitionSpec as P

NMOM = 7
ALPHA = 2.0 / 11.0
BETA = 13.0 / 11.0
EPS = 1e-06
TWO_PI = 2.0 * math.pi
RANGE = 2.0**40
COUNT = 196608.0
HIGHEST = lax.Precision.HIGHEST
F32 = jnp.float32
BF16 = jnp.bfloat16
VMEM_LIMIT = 56 * 1024 * 1024
LAY, STEP, FACE, GRAM, CARRY_X, CARRY_YZ, TURN = 4, 1, 4, 4, 2, 2, 4


def params(**extra):
    return pltpu.CompilerParams(vmem_limit_bytes=VMEM_LIMIT, **extra)


def link_of(rows, direction):
    def entry(part, a, b):
        lane = ((direction * 2 + part) * 3 + a) * 3 + b
        return jnp.broadcast_to(rows[:, lane : lane + 1], rows.shape)

    real = [[entry(0, a, b) for b in range(3)] for a in range(2)]
    imag = [[entry(1, a, b) for b in range(3)] for a in range(2)]
    third_real, third_imag = [], []
    for b in range(3):
        p, q = (b + 1) % 3, (b + 2) % 3
        first = real[0][p] * real[1][q] - imag[0][p] * imag[1][q]
        second = real[0][q] * real[1][p] - imag[0][q] * imag[1][p]
        third_real.append(first - second)
        first = real[0][p] * imag[1][q] + imag[0][p] * real[1][q]
        second = real[0][q] * imag[1][p] + imag[0][q] * real[1][p]
        third_imag.append(second - first)
    return [real + [third_real], imag + [third_imag]]


def forward(link, v):
    real, imag = [], []
    for a in range(3):
        r = i = None
        for b in range(3):
            x = link[0][a][b] * v[b] - link[1][a][b] * v[3 + b]
            y = link[0][a][b] * v[3 + b] + link[1][a][b] * v[b]
            r = x if r is None else r + x
            i = y if i is None else i + y
        real.append(r)
        imag.append(i)
    return real + imag


def backward(link, v):
    real, imag = [], []
    for a in range(3):
        r = i = None
        for b in range(3):
            x = link[0][b][a] * v[b] + link[1][b][a] * v[3 + b]
            y = link[0][b][a] * v[3 + b] - link[1][b][a] * v[b]
            r = x if r is None else r + x
            i = y if i is None else i + y
        real.append(r)
        imag.append(i)
    return real + imag


def add(first, second):
    return [a + b for a, b in zip(first, second)]


def lay_out(field, links):
    def kernel(field_ref, link_ref, out):
        for q in range(LAY):
            block = pl.program_id(0) * LAY + q
            for c in range(6):
                out[q, c * 128 : (c + 1) * 128, :] = field_ref[c, q * 128 : (q + 1) * 128, :]
            rows = [link_ref[:, pl.ds((4 * block + y + 31) % 32, 1), :].reshape(54, 32) for y in range(5)]
            out[q, 768:822, :] = jnp.concatenate(rows[1:], axis=1)
            out[q, 822:840, :] = jnp.concatenate([row[18:36] for row in rows[:4]], axis=1)

    return pl.pallas_call(
        kernel,
        grid=(8 // LAY,),
        in_specs=[
            pl.BlockSpec((6, 128 * LAY, 128), lambda q: (0, q, 0)),
            pl.BlockSpec((54, 32, 32), lambda q: (0, 0, 0)),
        ],
        out_specs=pl.BlockSpec((LAY, 840, 128), lambda q: (q, 0, 0)),
        out_shape=jax.ShapeDtypeStruct((8, 840, 128), F32),
        compiler_params=params(),
        cost_estimate=pl.CostEstimate(flops=3_000_000_000, bytes_accessed=7_000_000, transcendentals=0),
        name="lay_out",
    )(field, links)


def cell(ref, c, at, z=0):
    return ref[z, c * 128 + at.start : c * 128 + at.stop, :]


def cell_flat(ref, c, at):
    return ref[c * 128 + at.start : c * 128 + at.stop, :]


def interior(u, links, before, c0, c1, cp, name):
    first = links is None

    def kernel(*refs):
        if first:
            here, above, out, norm, link_ref, px, wx, py, pz = refs
            for zz in range(STEP):
                rows = jnp.concatenate([here[zz, 768:840, :], jnp.zeros((56, 128), F32)], axis=0)
                link_ref[zz] = rows.T
        else:
            here, above, link_ref, before_ref, out, norm, px, wx, py, pz = refs
        z = pl.program_id(0)
        inside = jnp.where(z < 8 // STEP - 1, 1.0, 0.0).astype(F32)

        @pl.when(z == 0)
        def _():
            norm[...] = jnp.zeros_like(norm)
            pz[...] = jnp.zeros_like(pz)

        total = jnp.zeros((8, 128), F32)
        for zz in range(STEP):
            for y in range(4):
                row = y * 32
                for c in range(6):
                    px[c] = pltpu.roll(cell(here, c, slice(row, row + 32), zz), 31, 0)
                for g in range(4):
                    at = slice(row + 8 * g, row + 8 * g + 8)
                    own = slice(8 * g, 8 * g + 8)
                    rows = link_ref[zz, at, :]
                    v = [cell(here, c, at, zz) for c in range(6)]
                    if not first:
                        for c in range(6):
                            total = total + v[c] * v[c]
                    link = link_of(rows, 0)
                    hop = forward(link, [px[c, own, :] for c in range(6)])
                    side = backward(link, v)
                    for c in range(6):
                        wx[c, own, :] = side[c]
                    if y < 3:
                        link = link_of(rows, 1)
                        up = slice(at.start + 32, at.stop + 32)
                        hop = add(hop, forward(link, [cell(here, c, up, zz) for c in range(6)]))
                        side = backward(link, v)
                    if y > 0:
                        hop = add(hop, [py[c, own, :] for c in range(6)])
                    if y < 3:
                        for c in range(6):
                            py[c, own, :] = side[c]
                    link = link_of(rows, 2)
                    far = forward(link, [cell(here, c, at, zz + 1) if zz < STEP - 1 else cell(above, c, at) for c in range(6)])
                    hop = add(hop, far) if zz < STEP - 1 else [a + inside * b for a, b in zip(hop, far)]
                    hop = add(hop, [pz[c, at, :] for c in range(6)])
                    side = backward(link, v)
                    for c in range(6):
                        pz[c, at, :] = side[c]
                        value = c0 * v[c] - c1 * hop[c]
                        if not first:
                            value = value - cp * cell(before_ref, c, at, zz)
                        out[zz, c * 128 + at.start : c * 128 + at.stop, :] = value
                for c in range(6):
                    spot = slice(c * 128 + row, c * 128 + row + 32)
                    out[zz, spot, :] = out[zz, spot, :] - c1 * pltpu.roll(wx[c], 1, 0)
        norm[...] = norm[...] + total

    block = pl.BlockSpec((STEP, 768, 128), lambda z: (z, 0, 0))
    next_block = pl.BlockSpec((1, 768, 128), lambda z: (jnp.minimum(STEP * (z + 1), 7), 0, 0))
    link_block = pl.BlockSpec((STEP, 128, 128), lambda z: (z, 0, 0))
    out_specs = [block, pl.BlockSpec((8, 128), lambda z: (0, 0))]
    out_shape = [jax.ShapeDtypeStruct((8, 768, 128), F32), jax.ShapeDtypeStruct((8, 128), F32)]
    if first:
        in_specs = [pl.BlockSpec((STEP, 840, 128), lambda z: (z, 0, 0)), next_block]
        operands = [u, u]
        out_specs.append(link_block)
        out_shape.append(jax.ShapeDtypeStruct((8, 128, 128), F32))
    else:
        in_specs = [block, next_block, link_block, block]
        operands = [u, u, links, before]
    return pl.pallas_call(
        kernel,
        grid=(8 // STEP,),
        in_specs=in_specs,
        out_specs=out_specs,
        out_shape=out_shape,
        scratch_shapes=[
            pltpu.VMEM((6, 32, 128), F32),
            pltpu.VMEM((6, 32, 128), F32),
            pltpu.VMEM((6, 32, 128), F32),
            pltpu.VMEM((6, 128, 128), F32),
        ],
        compiler_params=params(),
        cost_estimate=pl.CostEstimate(flops=12_000_000_000, bytes_accessed=12_000_000, transcendentals=0),
        name=name,
    )(*operands)


def boundary(partial, links, halo, z_links, c1, name):
    z_up, z_down, y_up, y_down = halo

    def kernel(part, link_ref, zu, zd, yu, yd, zl, out, y_low, y_high, z_low, z_high, turned):
        step = pl.program_id(0)

        def put(z, c, at, hop):
            spot = slice(c * 128 + at.start, c * 128 + at.stop)
            out[z, spot, :] = part[z, spot, :] - c1 * hop[c]

        def more(z, c, at, hop):
            spot = slice(c * 128 + at.start, c * 128 + at.stop)
            out[z, spot, :] = out[z, spot, :] - c1 * hop[c]

        for z in range(FACE):
            for g in range(4):
                own = slice(8 * g, 8 * g + 8)
                hop = backward(link_of(link_ref[z, own, :], 3), [yd[z, c, own, :] for c in range(6)])
                for c in range(6):
                    put(z, c, own, hop)
                at = slice(96 + 8 * g, 104 + 8 * g)
                hop = forward(link_of(link_ref[z, at, :], 1), [yu[z, c, own, :] for c in range(6)])
                for c in range(6):
                    put(z, c, at, hop)
            for c in range(6):
                spot = slice(c * 128 + 32, c * 128 + 96)
                out[z, spot, :] = part[z, spot, :]

        @pl.when(step == 0)
        def _():
            turned[...] = jnp.concatenate([zl[...], jnp.zeros((56, 128), F32)], axis=0).T
            for g in range(16):
                at = slice(8 * g, 8 * g + 8)
                hop = backward(link_of(turned[at, :], 2), [zd[c * 128 + at.start : c * 128 + at.stop, :] for c in range(6)])
                for c in range(6):
                    more(0, c, at, hop)
            z_low[...] = out[0]

        @pl.when(step == 8 // FACE - 1)
        def _():
            for g in range(16):
                at = slice(8 * g, 8 * g + 8)
                hop = forward(
                    link_of(link_ref[FACE - 1, at, :], 2), [zu[c * 128 + at.start : c * 128 + at.stop, :] for c in range(6)]
                )
                for c in range(6):
                    more(FACE - 1, c, at, hop)
            z_high[...] = out[FACE - 1]

        for z in range(FACE):
            for c in range(6):
                y_low[z, c] = out[z, c * 128 : c * 128 + 32, :]
                y_high[z, c] = out[z, c * 128 + 96 : c * 128 + 128, :]

    block = pl.BlockSpec((FACE, 768, 128), lambda z: (z, 0, 0))
    y_face = pl.BlockSpec((FACE, 6, 32, 128), lambda z: (z, 0, 0, 0))
    z_face = pl.BlockSpec((768, 128), lambda z: (0, 0))
    return pl.pallas_call(
        kernel,
        grid=(8 // FACE,),
        in_specs=[
            block,
            pl.BlockSpec((FACE, 128, 128), lambda z: (z, 0, 0)),
            z_face,
            z_face,
            y_face,
            y_face,
            pl.BlockSpec((72, 128), lambda z: (0, 0)),
        ],
        out_specs=(block, y_face, y_face, z_face, z_face),
        out_shape=(
            jax.ShapeDtypeStruct((8, 768, 128), F32),
            jax.ShapeDtypeStruct((8, 6, 32, 128), F32),
            jax.ShapeDtypeStruct((8, 6, 32, 128), F32),
            jax.ShapeDtypeStruct((768, 128), F32),
            jax.ShapeDtypeStruct((768, 128), F32),
        ),
        scratch_shapes=[pltpu.VMEM((128, 128), F32)],
        compiler_params=params(),
        cost_estimate=pl.CostEstimate(flops=6_000_000_000, bytes_accessed=9_000_000, transcendentals=0),
        name=name,
    )(partial, links, z_up, z_down, y_up, y_down, z_links)


def halves(value):
    high = value.astype(BF16)
    return high, (value - high.astype(F32)).astype(BF16)


def dot3(left, right):
    def dot(a, b):
        return jnp.dot(a, b, preferred_element_type=F32)

    return dot(left[0], right[0]) + (dot(left[0], right[1]) + dot(left[1], right[0]))


def columns(ref, z, part):
    return jnp.concatenate([cell(ref, 3 * part + a, slice(0, 128), z) for a in range(3)], axis=1)


def gram(u, first_norm, second_norm):
    def kernel(here, n1, n2, packed, turned, acc):
        step = pl.program_id(0)

        @pl.when(step == 0)
        def _():
            acc[...] = jnp.zeros_like(acc)

        for z in range(GRAM):
            for c in range(6):
                turned[z, c * 128 : (c + 1) * 128, :] = cell(here, c, slice(0, 128), z).T
        left = jnp.concatenate(
            [jnp.concatenate([columns(turned, z, part) for z in range(GRAM)], axis=1) for part in range(2)], axis=0
        )
        right = jnp.concatenate([here[z, 0:384, :] for z in range(GRAM)], axis=0)
        right = jnp.concatenate([right, jnp.concatenate([here[z, 384:768, :] for z in range(GRAM)], axis=0)], axis=1)
        acc[...] = acc[...] + dot3(halves(left), halves(right))

        @pl.when(step == 8 // GRAM - 1)
        def _():
            real = acc[0:128, 0:128] + acc[128:256, 128:256]
            imag = acc[0:128, 128:256] - acc[128:256, 0:128]
            row = lax.broadcasted_iota(jnp.int32, (128, 128), 0)
            column = lax.broadcasted_iota(jnp.int32, (128, 128), 1)
            packed[0:128, :] = jnp.where(column >= row, real, imag)
            packed[128:136, :] = n1[...]
            packed[136:144, :] = n2[...]

    fixed = pl.BlockSpec((8, 128), lambda z: (0, 0))
    return pl.pallas_call(
        kernel,
        grid=(8 // GRAM,),
        in_specs=[pl.BlockSpec((GRAM, 768, 128), lambda z: (z, 0, 0)), fixed, fixed],
        out_specs=(pl.BlockSpec((144, 128), lambda z: (0, 0)), pl.BlockSpec((GRAM, 768, 128), lambda z: (z, 0, 0))),
        out_shape=(jax.ShapeDtypeStruct((144, 128), F32), jax.ShapeDtypeStruct((8, 768, 128), F32)),
        scratch_shapes=[pltpu.VMEM((256, 256), F32)],
        compiler_params=params(),
        cost_estimate=pl.CostEstimate(flops=4_000_000_000, bytes_accessed=3_000_000, transcendentals=0),
        name="gram",
    )(u, first_norm, second_norm)


def put_halves(wide, zz, carry, slots):
    for a in range(3):
        for k in range(slots):
            for part in range(2):
                hi, lo = halves(carry[k, 3 * part + a])
                spot = (k * 2 + part) * 128
                wide[zz, a * 128 : (a + 1) * 128, spot : spot + 128] = hi
                wide[zz, 384 + a * 128 : 512 + a * 128, spot : spot + 128] = lo
                wide[zz, 768 + a * 128 : 896 + a * 128, spot : spot + 128] = hi


def add_hops(acc, turned, zz, carry, slots):
    left = jnp.concatenate([columns(turned, zz, part) for part in range(2)], axis=0)

    def summed(c):
        return carry[0, c] if slots == 1 else carry[0, c] + carry[1, c]

    right = jnp.concatenate(
        [jnp.concatenate([summed(a), summed(3 + a)], axis=1) for a in range(3)], axis=0
    )
    acc[...] = acc[...] + dot3(halves(left), halves(right))


def carry_x(u, turned, links):
    def kernel(here, turned, link_ref, wide, hops, px, carry, acc):
        z = pl.program_id(0)

        @pl.when(z == 0)
        def _():
            acc[...] = jnp.zeros_like(acc)

        for zz in range(CARRY_X):
            for y in range(4):
                row = y * 32
                for c in range(6):
                    px[c] = pltpu.roll(cell(here, c, slice(row, row + 32), zz), 31, 0)
                for g in range(4):
                    at = slice(row + 8 * g, row + 8 * g + 8)
                    own = slice(8 * g, 8 * g + 8)
                    found = forward(link_of(link_ref[zz, at, :], 0), [px[c, own, :] for c in range(6)])
                    for c in range(6):
                        carry[0, c, at, :] = found[c]
            put_halves(wide, zz, carry, 1)
            add_hops(acc, turned, zz, carry, 1)

        @pl.when(z == 8 // CARRY_X - 1)
        def _():
            hops[...] = acc[...]

    block = pl.BlockSpec((CARRY_X, 768, 128), lambda z: (z, 0, 0))
    return pl.pallas_call(
        kernel,
        grid=(8 // CARRY_X,),
        in_specs=[block, block, pl.BlockSpec((CARRY_X, 128, 128), lambda z: (z, 0, 0))],
        out_specs=(pl.BlockSpec((CARRY_X, 1152, 256), lambda z: (z, 0, 0)), pl.BlockSpec((256, 256), lambda z: (0, 0))),
        out_shape=(jax.ShapeDtypeStruct((8, 1152, 256), BF16), jax.ShapeDtypeStruct((256, 256), F32)),
        scratch_shapes=[
            pltpu.VMEM((6, 32, 128), F32),
            pltpu.VMEM((1, 6, 128, 128), F32),
            pltpu.VMEM((256, 256), F32),
        ],
        compiler_params=params(),
        cost_estimate=pl.CostEstimate(flops=7_000_000_000, bytes_accessed=8_000_000, transcendentals=0),
        name="carry_x",
    )(u, turned, links)


def carry_yz(u, turned, links, z_up, y_up, x_hops, packed_gram):
    def kernel(here, turned, above, link_ref, zu, yu, hops_ref, gram_ref, wide, packed, carry, acc):
        z = pl.program_id(0)
        last = z == 8 // CARRY_YZ - 1

        @pl.when(z == 0)
        def _():
            acc[...] = hops_ref[...]

        for zz in range(CARRY_YZ):
            for y in range(4):
                row = y * 32
                for g in range(4):
                    at = slice(row + 8 * g, row + 8 * g + 8)
                    own = slice(8 * g, 8 * g + 8)
                    rows = link_ref[zz, at, :]
                    if y < 3:
                        source = [cell(here, c, slice(at.start + 32, at.stop + 32), zz) for c in range(6)]
                    else:
                        source = [yu[zz, c, own, :] for c in range(6)]
                    found = forward(link_of(rows, 1), source)
                    for c in range(6):
                        carry[0, c, at, :] = found[c]
                    if zz < CARRY_YZ - 1:
                        source = [cell(here, c, at, zz + 1) for c in range(6)]
                    else:
                        source = [jnp.where(last, cell_flat(zu, c, at), cell(above, c, at)) for c in range(6)]
                    found = forward(link_of(rows, 2), source)
                    for c in range(6):
                        carry[1, c, at, :] = found[c]
            put_halves(wide, zz, carry, 2)
            add_hops(acc, turned, zz, carry, 2)

        @pl.when(last)
        def _():
            gram_real, gram_imag = hermitian(gram_ref[0:128, :])
            hop_real = acc[0:128, 0:128] + acc[128:256, 128:256]
            hop_imag = acc[0:128, 128:256] - acc[128:256, 0:128]
            real = 6.0 * gram_real - (hop_real + hop_real.T)
            imag = 6.0 * gram_imag - (hop_imag - hop_imag.T)
            row = lax.broadcasted_iota(jnp.int32, (128, 128), 0)
            column = lax.broadcasted_iota(jnp.int32, (128, 128), 1)
            packed[...] = jnp.where(column >= row, real, imag)

    return pl.pallas_call(
        kernel,
        grid=(8 // CARRY_YZ,),
        in_specs=[
            pl.BlockSpec((CARRY_YZ, 768, 128), lambda z: (z, 0, 0)),
            pl.BlockSpec((CARRY_YZ, 768, 128), lambda z: (z, 0, 0)),
            pl.BlockSpec((1, 768, 128), lambda z: (jnp.minimum(CARRY_YZ * (z + 1), 7), 0, 0)),
            pl.BlockSpec((CARRY_YZ, 128, 128), lambda z: (z, 0, 0)),
            pl.BlockSpec((768, 128), lambda z: (0, 0)),
            pl.BlockSpec((CARRY_YZ, 6, 32, 128), lambda z: (z, 0, 0, 0)),
            pl.BlockSpec((256, 256), lambda z: (0, 0)),
            pl.BlockSpec((144, 128), lambda z: (0, 0)),
        ],
        out_specs=(pl.BlockSpec((CARRY_YZ, 1152, 512), lambda z: (z, 0, 0)), pl.BlockSpec((128, 128), lambda z: (0, 0))),
        out_shape=(jax.ShapeDtypeStruct((8, 1152, 512), BF16), jax.ShapeDtypeStruct((128, 128), F32)),
        scratch_shapes=[pltpu.VMEM((2, 6, 128, 128), F32), pltpu.VMEM((256, 256), F32)],
        compiler_params=params(),
        cost_estimate=pl.CostEstimate(flops=12_000_000_000, bytes_accessed=16_000_000, transcendentals=0),
        name="carry_yz",
    )(u, turned, u, links, z_up, y_up, x_hops, packed_gram)


def elementals(core, z, turned_u, right_x, right_yz, phases, first, count, extra, spare, name):
    def kernel(core_ref, z_ref, here, rx, ryz, phase, *refs):
        kept, given, left, acc = refs[-4:]
        step = pl.program_id(0)
        own = core_ref[0] == 0

        @pl.when(step == 0)
        def _():
            acc[...] = jnp.zeros_like(acc)

        turned = [[here[zz, c * 128 : (c + 1) * 128, :] for c in range(6)] for zz in range(2)]
        minus = [[-turned[zz][a] for a in range(3)] for zz in range(2)]

        def build(m):
            mode = 2 * (first + m)
            for zz in range(2):
                cosine = phase[zz, mode : mode + 1, :]
                sine = phase[zz, mode + 1 : mode + 2, :]
                for a in range(3):
                    real, imag = turned[zz][a], turned[zz][3 + a]
                    spot = zz * 1152 + a * 128
                    pair = (real * cosine - imag * sine, minus[zz][a] * sine - imag * cosine)
                    for part in range(2):
                        hi, lo = halves(pair[part])
                        rows = slice(m * 256 + part * 128, m * 256 + part * 128 + 128)
                        left[rows, spot : spot + 128] = hi
                        left[rows, spot + 384 : spot + 512] = hi
                        left[rows, spot + 768 : spot + 896] = lo

        def multiply(low, high):
            done = slice(low * 256, high * 256)
            found = jnp.dot(left[done, :], rx[...].reshape(2304, 256), preferred_element_type=F32)
            acc[done, 0:256] = acc[done, 0:256] + found
            found = jnp.dot(left[done, :], ryz[...].reshape(2304, 512), preferred_element_type=F32)
            acc[done, 256:768] = acc[done, 256:768] + found

        for m in range(2):
            build(m)
        for m in range(2, count):
            build(m)
        for low in range(0, count, 2):
            multiply(low, min(low + 2, count))

        @pl.when(step == 3)
        def _():
            def share(lanes, value):
                for chip in range(16):
                    low, high = value[chip * 8 : chip * 8 + 4], value[chip * 8 + 4 : chip * 8 + 8]
                    kept[chip, :, lanes] = jnp.where(own, low, high)
                    given[chip, :, lanes] = jnp.where(own, high, low)

            width = spare * 128
            lanes = slice(count * 768, count * 768 + width)
            share(lanes, jnp.zeros((128, width), F32) if extra is None else refs[0][...])
            turn = halves(jnp.concatenate([z_ref[0].T, z_ref[1].T], axis=0))
            for m in range(count):
                real, imag = slice(m * 256, m * 256 + 128), slice(m * 256 + 128, m * 256 + 256)
                for k in range(3):
                    one, two = slice(256 * k, 256 * k + 128), slice(256 * k + 128, 256 * k + 256)
                    raw = [acc[real, one] - acc[imag, two], acc[real, two] + acc[imag, one]]
                    found = dot3(turn, halves(jnp.concatenate(raw, axis=1)))
                    place = (m * 3 + k) * 256
                    share(slice(place, place + 128), found[0:128, 0:128] + found[128:256, 128:256])
                    share(slice(place + 128, place + 256), found[0:128, 128:256] - found[128:256, 0:128])

    shape = (16, 4, count * 768 + spare * 128)
    return pl.pallas_call(
        kernel,
        grid=(4,),
        in_specs=[
            pl.BlockSpec(memory_space=pltpu.SMEM),
            pl.BlockSpec((2, 128, 128), lambda z: (0, 0, 0)),
            pl.BlockSpec((2, 768, 128), lambda z: (z, 0, 0)),
            pl.BlockSpec((2, 1152, 256), lambda z: (z, 0, 0)),
            pl.BlockSpec((2, 1152, 512), lambda z: (z, 0, 0)),
            pl.BlockSpec((2, 14, 128), lambda z: (z, 0, 0)),
        ]
        + [pl.BlockSpec((128, 128), lambda z: (0, 0))] * (extra is not None),
        out_specs=[pl.BlockSpec(shape, lambda z: (0, 0, 0))] * 2,
        out_shape=[jax.ShapeDtypeStruct(shape, F32)] * 2,
        scratch_shapes=[
            pltpu.VMEM((count * 256, 2304), BF16),
            pltpu.VMEM((count * 256, 768), F32),
        ],
        compiler_params=params(),
        cost_estimate=pl.CostEstimate(flops=5_500_000_000 * count, bytes_accessed=16_000_000, transcendentals=0),
        name=name,
    )(core, z, turned_u, right_x, right_yz, phases, *([] if extra is None else [extra]))


def hermitian(packed):
    row = lax.broadcasted_iota(jnp.int32, (128, 128), 0)
    column = lax.broadcasted_iota(jnp.int32, (128, 128), 1)
    diagonal = jnp.where(column == row, packed, 0.0)
    upper = jnp.where(column > row, packed, 0.0)
    lower = jnp.where(column < row, packed, 0.0)
    return upper + upper.T + diagonal, lower - lower.T


def complex_dot(left, right):
    top = jnp.concatenate([left[0], -left[1]], axis=1)
    bottom = jnp.concatenate([left[1], left[0]], axis=1)
    both = dot3(halves(jnp.concatenate([top, bottom], axis=0)), halves(jnp.concatenate([right[0], right[1]], axis=0)))
    return both[0:128], both[128:256]


def newton(total):
    def kernel(ref, z_out):
        row = lax.broadcasted_iota(jnp.int32, (128, 128), 0)
        column = lax.broadcasted_iota(jnp.int32, (128, 128), 1)
        identity = jnp.where(row == column, 1.0, 0.0).astype(F32)
        g_real, g_imag = hermitian(ref[0:128, :])
        shrink = 1.0 / (RANGE * RANGE)
        n1 = jnp.sum(ref[128:136, :], axis=0, keepdims=True) * shrink / COUNT
        n2 = jnp.sum(ref[136:144, :], axis=0, keepdims=True) * shrink / COUNT
        n3 = jnp.sum(jnp.where(row == column, g_real, 0.0), axis=0, keepdims=True) * shrink / COUNT
        scale = lax.rsqrt(n1 + EPS)
        scale = scale * lax.rsqrt(scale * scale * n2 + EPS)
        scale = scale * lax.rsqrt(scale * scale * n3 + EPS)
        scale = jnp.broadcast_to(scale * (1.0 / RANGE), (128, 128))
        side = scale.T
        y = (side * g_real * scale / COUNT, side * g_imag * scale / COUNT)
        inverse = None
        for step in range(3):
            middle = y if inverse is None else complex_dot(inverse, y)
            factor = (1.5 * identity - 0.5 * middle[0], -0.5 * middle[1])
            if step < 2:
                y = complex_dot(y, factor)
            inverse = factor if inverse is None else complex_dot(factor, inverse)
        z_out[0] = side * inverse[0]
        z_out[1] = side * inverse[1]

    return pl.pallas_call(
        kernel,
        out_shape=jax.ShapeDtypeStruct((2, 128, 128), F32),
        compiler_params=params(),
        cost_estimate=pl.CostEstimate(flops=5_000_000_000, bytes_accessed=300_000, transcendentals=0),
        name="newton",
    )(total)


def rayleigh(total, z):
    def kernel(ref, z_ref, out):
        h = hermitian(ref[...])
        inverse = (z_ref[0], z_ref[1])
        half = complex_dot(h, inverse)
        full = complex_dot((inverse[0].T, -inverse[1].T), half)
        out[0] = full[0] / COUNT
        out[1] = full[1] / COUNT

    return pl.pallas_call(
        kernel,
        out_shape=jax.ShapeDtypeStruct((2, 128, 128), F32),
        compiler_params=params(),
        cost_estimate=pl.CostEstimate(flops=3_000_000_000, bytes_accessed=300_000, transcendentals=0),
        name="rayleigh",
    )(total, z)


def rotate(z, blocks):
    def kernel(z_ref, ref, out):
        top = jnp.concatenate([z_ref[0], z_ref[1]], axis=1)
        bottom = jnp.concatenate([-z_ref[1], z_ref[0]], axis=1)
        right = halves(jnp.concatenate([top, bottom], axis=0))
        for a in range(3):
            real, imag = slice(a * 128, a * 128 + 128), slice(384 + a * 128, 512 + a * 128)
            left = jnp.concatenate(
                [jnp.concatenate([ref[q, real, :], ref[q, imag, :]], axis=1) for q in range(TURN)], axis=0
            )
            found = dot3(halves(left), right)
            out[a] = found[:, 0:128]
            out[3 + a] = found[:, 128:256]

    return pl.pallas_call(
        kernel,
        grid=(8 // TURN,),
        in_specs=[
            pl.BlockSpec((2, 128, 128), lambda i: (0, 0, 0)),
            pl.BlockSpec((TURN, 768, 128), lambda i: (i, 0, 0)),
        ],
        out_specs=pl.BlockSpec((6, 128 * TURN, 128), lambda i: (0, i, 0)),
        out_shape=jax.ShapeDtypeStruct((6, 1024, 128), F32),
        compiler_params=params(),
        cost_estimate=pl.CostEstimate(flops=5_000_000_000, bytes_accessed=7_000_000, transcendentals=0),
        name="rotate",
    )(z, blocks)


def ring_pairs(step):
    return [(z * 8 + r, z * 8 + (r + step) % 8) for z in range(4) for r in range(8)]


def z_pairs(step):
    return [(i, (i + 8 * step) % 32) for i in range(32)]


def y_pairs(step):
    return ring_pairs(2 * step)


RINGS = [[z * 8 + r for r in range(8)] for z in range(4)]
CORES = [[2 * chip + core for chip in range(16)] for core in range(2)]
CORE_PAIRS = [(i, i ^ 1) for i in range(32)]


def move(value, pairs):
    return lax.ppermute(value, "sa", pairs)


def trade(value, groups=None):
    return lax.all_to_all(value, "sa", 0, 0, axis_index_groups=groups, tiled=True)


def spread(value, pairs):
    return [move(value, pairs(step)) for step in (2, 1, -1)]


def gathered(value, parts):
    return (value + parts[0]) + (parts[1] + parts[2])


def local(start, links, momenta, displace):
    device = lax.axis_index("sa")
    ring = device % 8

    u = trade(lay_out(start.reshape(6, 1024, 128), links.reshape(54, 32, 32)), RINGS)

    zs = (device // 8) * 8 + jnp.arange(8, dtype=jnp.int32)[None, :, None, None]
    ys = ring * 4 + jnp.arange(4, dtype=jnp.int32)[None, None, :, None]
    xs = jnp.arange(32, dtype=jnp.int32)[None, None, None, :]
    along_x = momenta[:, 0][:, None, None, None]
    along_y = momenta[:, 1][:, None, None, None]
    along_z = momenta[:, 2][:, None, None, None]
    angles = TWO_PI * (
        (along_x * xs % 32).astype(F32) / 32
        + (along_y * ys % 32).astype(F32) / 32
        + (along_z * zs % 32).astype(F32) / 32
    )
    angles = angles.reshape(NMOM, 8, 128)
    phases = jnp.stack([jnp.cos(angles), jnp.sin(angles)], axis=1).reshape(2 * NMOM, 8, 128)
    phases = jnp.transpose(phases, (1, 0, 2))

    cells = u[:, 0:768].reshape(8, 6, 128, 128)
    z_low, z_high = u[0, 0:768], u[7]
    y_low, y_high = cells[:, :, 0:32], cells[:, :, 96:128]
    before = mesh_links = z_links = None
    norms = []
    for step in range(3):
        weight = (1.0 if step else RANGE) * (2.0 if step else 1.0)
        z_down = move(z_high, z_pairs(1))
        z_up = move(z_low, z_pairs(-1))
        y_down = move(y_high, ring_pairs(1))
        y_up = move(y_low, ring_pairs(-1))
        if step == 0:
            z_links = z_down[768:840]
        found = interior(
            u,
            mesh_links,
            before,
            weight * (6.0 * ALPHA - BETA),
            weight * ALPHA,
            RANGE if step == 1 else 1.0,
            f"interior_{step}",
        )
        if step == 0:
            mesh_links = found[2]
        norms.append(found[1])
        fresh, y_low, y_high, z_low, z_high = boundary(
            found[0], mesh_links, (z_up, z_down, y_up, y_down), z_links, weight * ALPHA, f"boundary_{step}"
        )
        before, u = u, fresh

    z_up = move(z_low, z_pairs(-1))
    y_up = move(y_low, ring_pairs(-1))
    packed_gram, turned = gram(u, norms[1], norms[2])
    shared = packed_gram + move(packed_gram, CORE_PAIRS)
    ring_parts = spread(shared, y_pairs)
    right_x, x_hops = carry_x(u, turned, mesh_links)
    ring_parts, x_hops, z_up, y_up, u = lax.optimization_barrier((ring_parts, x_hops, z_up, y_up, u))
    back = trade(u, RINGS)
    shared = gathered(shared, ring_parts)
    z_parts = spread(shared, z_pairs)
    right_yz, packed_h = carry_yz(u, turned, mesh_links, z_up, y_up, x_hops, packed_gram)
    z_parts, packed_h = lax.optimization_barrier((z_parts, packed_h))
    total_gram = gathered(shared, z_parts)
    z = newton(total_gram)
    core = device % 2
    where = core.reshape(1).astype(jnp.int32)
    kept, given = elementals(where, z, turned, right_x, right_yz, phases, 0, 4, packed_h, 1, "elementals_0")
    first = kept + move(given, CORE_PAIRS)
    first, back, turned = lax.optimization_barrier((first, back, turned))
    first = jnp.sum(trade(first, CORES), axis=0)
    kept, given = elementals(where, z, turned, right_x, right_yz, phases, 4, 3, None, 2, "elementals_1")
    first, kept, given = lax.optimization_barrier((first, kept, given))
    share = jnp.broadcast_to(first[:, 3072:], (16, 4, 128))
    given = lax.dynamic_update_slice(given, share, (0, 0, 2432))
    second = lax.dynamic_update_slice(kept, share, (0, 0, 2304)) + move(given, CORE_PAIRS)
    second, back = lax.optimization_barrier((second, back))
    second = trade(second, CORES)
    mine, others = second[:, :, 2304:2432], second[:, :, 2432:]
    low, high = jnp.where(core == 0, mine, others), jnp.where(core == 0, others, mine)
    total = jnp.stack([low, high], axis=1).reshape(128, 128)
    sums = [first[:, :3072], jnp.sum(second[:, :, :2304], axis=0)]
    ritz = rayleigh(total, z)
    basis = rotate(z, back).reshape(start.shape)

    rows = jnp.concatenate([part.reshape(4, -1, 2, 128) for part in sums], axis=1)
    real, imag = rows[:, :, 0].reshape(-1, 128), rows[:, :, 1].reshape(-1, 128)
    left = jnp.concatenate([real, imag], axis=1)
    top = jnp.concatenate([z[0], z[1]], axis=1)
    bottom = jnp.concatenate([-z[1], z[0]], axis=1)
    phi = jnp.dot(left, jnp.concatenate([top, bottom], axis=0), precision=HIGHEST)
    phi = (phi * (1.0 / math.sqrt(32768.0))).reshape(4, NMOM, 3, 2, 128)
    slots = displace[:, None] == jnp.arange(3, dtype=displace.dtype)[None, :]
    phi = jnp.sum(jnp.where(slots[None, None, :, :, None, None], phi[:, :, None], 0.0), axis=3)
    return (basis, ritz, phi)


def solution(mesh):
    in_specs = (
        P("ta", None, "sa", None, None, None),
        P("ta", None, None, None, "sa", None, None),
        P(),
        P(),
    )
    out_specs = (
        P("ta", None, "sa", None, None, None),
        P("ta", None, None),
        P("sa", "ta", None, None, None),
    )
    return jax.shard_map(local, mesh=mesh, in_specs=in_specs, out_specs=out_specs, check_vma=False)
```

profile of v0, /device:TPU:0, one launch (start us, length us, event | category | flops | bytes accessed | tf_op | source)
XLA Modules:
  0.0 264.0 jit_solution(15959816981089789531)
XLA Ops:
  0.6 4.1 %lay_out.1 = f32[8,840,128]{2,1,0:T(8,128)} custom-call(f32[6,1024,128]{2,1,0:T(8,128)} %bitcast.37, f32[54,32,32]{2,1,0:T(8,128)} %bitcast.38), custom_call_target="tpu_custom_call" | custom-call | flops 3000000000 | bytes 7000000 | tf_op jit(solution)/shard_map/lay_out/pallas_call | solution.py:89
  4.7 4.7 %all-to-all-start = ((f32[8,840,128]{2,1,0:T(8,128)}), f32[8,840,128]{2,1,0:T(8,128)S(1)}, u32[]{:S(2)}, u32[]{:S(2)}) async-start(f32[8,840,128]{2,1,0:T(8,128)} %lay_out.1), calls=%async_computation | async-start | bytes 6881280 | tf_op jit(solution)/shard_map/all_to_all | solution.py:692
  9.9 0.2 fusion.11
  10.1 41.0 %all-to-all-done.refs_0_.refs_1_.refs_3_ = f32[8,840,128]{2,1,0:T(8,128)S(1)} async-done(((f32[8,840,128]{2,1,0:T(8,128)}), f32[8,840,128]{2,1,0:T(8,128)S(1)}, u32[]{:S(2)}, u32[]{:S(2)}) %all-to-all-start) | async-done | bytes 3440672 | tf_op jit(solution)/shard_map/all_to_all | solution.py:692
  51.1 2.0 collective-permute-start.1
  53.0 0.2 slice.79
  53.4 0.1 collective-permute-start.2
  53.5 0.4 collective-permute-start.3
  53.9 2.9 %collective-permute-start = (f32[768,128]{1,0:T(8,128)S(1)}, f32[768,128]{1,0:T(8,128)S(1)}, u32[]{:S(2)}, u32[]{:S(2)}) collective-permute-start(f32[768,128]{1,0:T(8,128)S(1)} %slice_bitcast_fusion.1), channel_id=1, source_target_pairs={{0,24},{1,25},{2,26},{3,27},{4,28},{5,29},{6,30},{7,31},{8,0},{9,1... | collective-permute-start | bytes 1179656 | tf_op jit(solution)/shard_map/ppermute | solution.py:688
  56.9 14.4 %interior_0.1 = (f32[8,768,128]{2,1,0:T(8,128)}, f32[8,128]{1,0:T(8,128)}, f32[8,128,128]{2,1,0:T(8,128)}) custom-call(f32[8,840,128]{2,1,0:T(8,128)} %copy-done, f32[8,840,128]{2,1,0:T(8,128)} %copy-done), custom_call_target="tpu_custom_call" | custom-call | flops 12000000000 | bytes 12000000 | tf_op jit(solution)/shard_map/interior_0/pallas_call | solution.py:189
  71.3 0.7 slice.82.zl
  72.1 0.6 copy-done.16
  72.7 0.3 copy-done.7
  73.0 0.3 copy-done.10
  73.3 6.5 %boundary_0.1 = (f32[8,768,128]{2,1,0:T(8,128)}, f32[8,6,32,128]{3,2,1,0:T(8,128)}, f32[8,6,32,128]{3,2,1,0:T(8,128)}, f32[768,128]{1,0:T(8,128)}, f32[768,128]{1,0:T(8,128)}) custom-call(f32[8,768,128]{2,1,0:T(8,128)} %get-tuple-element.51.part, f32[8,128,128]{2,1,0:T(8,128)} %get-tuple-element.52.link_ref.refs_2_, f32[768,128]{1,0:T(8,128)} %copy-done.16, ...), custom_call_target="tpu_custom_call" | custom-call | flops 6000000000 | bytes 9000000 | tf_op jit(solution)/shard_map/boundary_0/pallas_call | solution.py:264
  79.8 1.9 collective-permute-start.6
  81.6 1.7 collective-permute-start.4
  83.3 0.3 collective-permute-start.5
  83.6 14.7 %interior_1.1 = (f32[8,768,128]{2,1,0:T(8,128)}, f32[8,128]{1,0:T(8,128)}) custom-call(f32[8,768,128]{2,1,0:T(8,128)} %get-tuple-element.53.refs_0_.refs_1_.refs_3_, f32[8,768,128]{2,1,0:T(8,128)} %get-tuple-element.53.refs_0_.refs_1_.refs_3_, f32[8,128,128]{2,1,0:T(8,128)} %get-tuple-element.52.link_ref.refs_2_, f32[8,840,128]{2,1,0:T(8,128)} %copy-done), custom_call_target="tpu_custom_call" | custom-call | flops 12000000000 | bytes 12000000 | tf_op jit(solution)/shard_map/interior_1/pallas_call | solution.py:189
  98.5 0.7 copy-done.15
  99.3 0.3 copy-done.8
  99.6 0.3 copy-done.11
  99.8 6.4 %boundary_1.1 = (f32[8,768,128]{2,1,0:T(8,128)}, f32[8,6,32,128]{3,2,1,0:T(8,128)}, f32[8,6,32,128]{3,2,1,0:T(8,128)}, f32[768,128]{1,0:T(8,128)}, f32[768,128]{1,0:T(8,128)}) custom-call(f32[8,768,128]{2,1,0:T(8,128)} %get-tuple-element.54.part, f32[8,128,128]{2,1,0:T(8,128)} %get-tuple-element.52.link_ref.refs_2_, f32[768,128]{1,0:T(8,128)} %copy-done.15, ...), custom_call_target="tpu_custom_call" | custom-call | flops 6000000000 | bytes 9000000 | tf_op jit(solution)/shard_map/boundary_1/pallas_call | solution.py:264
  106.3 2.4 collective-permute-start.10
  108.7 2.9 %collective-permute-start.8 = (f32[768,128]{1,0:T(8,128)}, f32[768,128]{1,0:T(8,128)S(1)}, u32[]{:S(2)}, u32[]{:S(2)}) collective-permute-start(f32[768,128]{1,0:T(8,128)} %get-tuple-element.61), channel_id=1, source_target_pairs={{0,24},{1,25},{2,26},{3,27},{4,28},{5,29},{6,30},{7,31},{8,0},{9,1... | collective-permute-start | bytes 1179656 | tf_op jit(solution)/shard_map/ppermute | solution.py:688
  111.6 14.6 %interior_2.1 = (f32[8,768,128]{2,1,0:T(8,128)}, f32[8,128]{1,0:T(8,128)}) custom-call(f32[8,768,128]{2,1,0:T(8,128)} %get-tuple-element.59.refs_0_.refs_1_, f32[8,768,128]{2,1,0:T(8,128)} %get-tuple-element.59.refs_0_.refs_1_, f32[8,128,128]{2,1,0:T(8,128)} %get-tuple-element.52.link_ref.refs_2_, f32[8,768,128]{2,1,0:T(8,128)} %get-tuple-element.53.refs_0_.refs_1_.refs_3_), custom_call_target="tpu_custom_call" | custom-call | flops 12000000000 | bytes 12000000 | tf_op jit(solution)/shard_map/interior_2/pallas_call | solution.py:189
  126.3 0.7 copy-done.14
  127.1 0.3 copy-done.6
  127.4 0.2 copy-done.9
  127.6 6.4 %boundary_2.1 = (f32[8,768,128]{2,1,0:T(8,128)}, f32[8,6,32,128]{3,2,1,0:T(8,128)}, f32[8,6,32,128]{3,2,1,0:T(8,128)}, f32[768,128]{1,0:T(8,128)}, f32[768,128]{1,0:T(8,128)}) custom-call(f32[8,768,128]{2,1,0:T(8,128)} %get-tuple-element.60.part, f32[8,128,128]{2,1,0:T(8,128)} %get-tuple-element.52.link_ref.refs_2_, f32[768,128]{1,0:T(8,128)} %copy-done.14, ...), custom_call_target="tpu_custom_call" | custom-call | flops 6000000000 | bytes 9000000 | tf_op jit(solution)/shard_map/boundary_2/pallas_call | solution.py:264
  134.0 2.7 %collective-permute-start.17 = (f32[8,6,32,128]{3,2,1,0:T(8,128)}, f32[8,6,32,128]{3,2,1,0:T(8,128)S(1)}, u32[]{:S(2)}, u32[]{:S(2)}) collective-permute-start(f32[8,6,32,128]{3,2,1,0:T(8,128)} %get-tuple-element.72), channel_id=1, source_target_pairs={{0,7},{1,0},{2,1},{3,2},{4,3},{5,4},{6,5},{7,6},{8,15},{9,8},{10,9... | collective-permute-start | bytes 2359304 | tf_op jit(solution)/shard_map/ppermute | solution.py:688
  136.7 4.7 %gram.1 = (f32[144,128]{1,0:T(8,128)}, f32[8,768,128]{2,1,0:T(8,128)}) custom-call(f32[8,768,128]{2,1,0:T(8,128)} %get-tuple-element.76.here.above, f32[8,128]{1,0:T(8,128)} %get-tuple-element.66.n1, f32[8,128]{1,0:T(8,128)} %get-tuple-element.67.n2), custom_call_target="tpu_custom_call" | custom-call | flops 4000000000 | bytes 3000000 | tf_op jit(solution)/shard_map/gram/pallas_call | solution.py:336
  141.4 0.6 copy.20
  142.1 2.9 %collective-permute-start.16 = (f32[768,128]{1,0:T(8,128)S(1)}, f32[768,128]{1,0:T(8,128)S(1)}, u32[]{:S(2)}, u32[]{:S(2)}) collective-permute-start(f32[768,128]{1,0:T(8,128)S(1)} %copy-done.12), channel_id=1, source_target_pairs={{0,24},{1,25},{2,26},{3,27},{4,28},{5,29},{6,30},{7,31},{8,0},{9,1... | collective-permute-start | bytes 1179656 | tf_op jit(solution)/shard_map/ppermute | solution.py:688
  145.0 0.9 add.136
  146.0 1.3 collective-permute-start.14
  147.3 2.0 collective-permute-start.15
  149.3 8.6 %carry_x.1 = (bf16[8,1152,256]{2,1,0:T(8,128)(2,1)}, f32[256,256]{1,0:T(8,128)}) custom-call(f32[8,768,128]{2,1,0:T(8,128)} %get-tuple-element.76.here.above, f32[8,768,128]{2,1,0:T(8,128)} %get-tuple-element.90.turned.here, f32[8,128,128]{2,1,0:T(8,128)} %get-tuple-element.52.link_ref.refs_2_), custom_call_target="tpu_custom_call" | custom-call | flops 7000000000 | bytes 8000000 | tf_op jit(solution)/shard_map/carry_x/pallas_call | solution.py:399
  158.1 0.6 copy-done.13
  158.8 1.1 collective-permute-start.19
  159.8 2.2 collective-permute-start.20
  162.0 3.9 %all-to-all-start.1 = ((f32[8,768,128]{2,1,0:T(8,128)}), f32[8,768,128]{2,1,0:T(8,128)S(1)}, u32[]{:S(2)}, u32[]{:S(2)}) async-start(f32[8,768,128]{2,1,0:T(8,128)} %get-tuple-element.76.here.above), calls=%async_computation.1 | async-start | bytes 6291456 | tf_op jit(solution)/shard_map/all_to_all | solution.py:692
  165.9 13.0 %carry_yz.1 = (bf16[8,1152,512]{2,1,0:T(8,128)(2,1)}, f32[128,128]{1,0:T(8,128)}) custom-call(f32[8,768,128]{2,1,0:T(8,128)} %get-tuple-element.76.here.above, f32[8,768,128]{2,1,0:T(8,128)} %get-tuple-element.90.turned.here, f32[8,768,128]{2,1,0:T(8,128)} %get-tuple-element.76.here.above, f32[8,128,128]{2,1,0:T(8,128)} %get-tuple-element.52.link_ref.refs_2_, ...), custom_call_target="tpu_custom_call" | custom-call | flops 12000000000 | bytes 16000000 | tf_op jit(solution)/shard_map/carry_yz/pallas_call | solution.py:460
  178.9 0.7 add_add_fusion.ref
  179.6 3.1 %newton.1.z_ref = f32[2,128,128]{2,1,0:T(8,128)} custom-call(f32[144,128]{1,0:T(8,128)} %add_add_fusion.ref), custom_call_target="tpu_custom_call" | custom-call | flops 5000000000 | bytes 300000 | tf_op jit(solution)/shard_map/newton/pallas_call | solution.py:614
  182.7 21.2 %elementals_0.1 = (f32[16,4,3200]{2,1,0:T(4,128)}, f32[16,4,3200]{2,1,0:T(4,128)}) custom-call(s32[1]{0:T(128)} %bitcast.5.core_ref, f32[2,128,128]{2,1,0:T(8,128)} %newton.1.z_ref, f32[8,768,128]{2,1,0:T(8,128)} %get-tuple-element.90.turned.here, bf16[8,1152,256]{2,1,0:T(8,128)(2,1)} %get-tuple-element.84.rx, bf16[8,1152,512]{2,1,0:T(8,128)(2,1)} %get-tuple-element.85.ryz, ...), custom_call_target="tpu_custom_call" | custom-call | flops 22000001024 | bytes 16000000 | tf_op jit(solution)/shard_map/elementals_0/pallas_call | solution.py:548
  203.9 0.2 collective-permute-start.21
  204.1 2.4 collective-permute-done.21
  206.5 2.3 add.159
  208.7 1.6 copy-done.1
  210.4 5.7 %all-to-all-start.2 = ((f32[16,4,3200]{2,1,0:T(4,128)}), f32[16,4,3200]{2,1,0:T(4,128)S(1)}, u32[]{:S(2)}, u32[]{:S(2)}) async-start(f32[16,4,3200]{2,1,0:T(4,128)} %add.159), calls=%async_computation.2 | async-start | bytes 1638400 | tf_op jit(solution)/shard_map/all_to_all | solution.py:692
  216.1 17.7 %elementals_1.1 = (f32[16,4,2560]{2,1,0:T(4,128)}, f32[16,4,2560]{2,1,0:T(4,128)}) custom-call(s32[1]{0:T(128)} %bitcast.5.core_ref, f32[2,128,128]{2,1,0:T(8,128)} %newton.1.z_ref, f32[8,768,128]{2,1,0:T(8,128)} %get-tuple-element.90.turned.here, bf16[8,1152,256]{2,1,0:T(8,128)(2,1)} %get-tuple-element.84.rx, bf16[8,1152,512]{2,1,0:T(8,128)(2,1)} %get-tuple-element.85.ryz, ...), custom_call_target="tpu_custom_call" | custom-call | flops 16499999744 | bytes 16000000 | tf_op jit(solution)/shard_map/elementals_1/pallas_call | solution.py:548
  234.0 0.7 broadcast_dynamic-update-slice_fusion
  234.7 2.2 collective-permute-done.22
  236.9 2.1 add.160
  239.1 7.2 %all-to-all-start.3 = ((f32[16,4,2560]{2,1,0:T(4,128)}), f32[16,4,2560]{2,1,0:T(4,128)S(1)}, u32[]{:S(2)}, u32[]{:S(2)}) async-start(f32[16,4,2560]{2,1,0:T(4,128)} %add.160), calls=%async_computation.3 | async-start | bytes 1310720 | tf_op jit(solution)/shard_map/all_to_all | solution.py:692
  246.4 4.2 %rotate.1 = f32[6,1024,128]{2,1,0:T(8,128)} custom-call(f32[2,128,128]{2,1,0:T(8,128)} %newton.1.z_ref, f32[8,768,128]{2,1,0:T(8,128)} %copy-done.1), custom_call_target="tpu_custom_call" | custom-call | flops 5000000000 | bytes 7000000 | tf_op jit(solution)/shard_map/rotate/pallas_call | solution.py:655
  250.5 9.0 %all-to-all-done.3 = f32[16,4,2560]{2,1,0:T(4,128)S(1)} async-done(((f32[16,4,2560]{2,1,0:T(4,128)}), f32[16,4,2560]{2,1,0:T(4,128)S(1)}, u32[]{:S(2)}, u32[]{:S(2)}) %all-to-all-start.3) | async-done | bytes 655392 | tf_op jit(solution)/shard_map/all_to_all | solution.py:692
  259.6 0.2 slice_reduce_fusion.2
  259.9 0.3 convolution_multiply_fusion
  260.3 0.1 select_reduce_fusion
  260.4 0.7 copy.16
  261.1 0.6 copy.13
  261.8 2.2 rayleigh.1
  (89 shorter events, 1.8 us)
Async XLA Ops:
  4.7 4.7 %copy-start.4 = (s32[7,3]{0,1:T(4,128)S(1)}, s32[7,3]{0,1:T(4,128)}, u32[]{:S(2)}) copy-start(s32[7,3]{0,1:T(4,128)} %param.6) | copy-start | bytes 256
  4.7 46.3 %all-to-all-start = ((f32[8,840,128]{2,1,0:T(8,128)}), f32[8,840,128]{2,1,0:T(8,128)S(1)}, u32[]{:S(2)}, u32[]{:S(2)}) async-start(f32[8,840,128]{2,1,0:T(8,128)} %lay_out.1), calls=%async_computation | async-start | bytes 6881280 | tf_op jit(solution)/shard_map/all_to_all | solution.py:692
  51.0 2.9 %copy-start = (f32[8,840,128]{2,1,0:T(8,128)}, f32[8,840,128]{2,1,0:T(8,128)S(1)}, u32[]{:S(2)}) copy-start(f32[8,840,128]{2,1,0:T(8,128)S(1)} %all-to-all-done.refs_0_.refs_1_.refs_3_) | copy-start | bytes 10321924
  51.1 20.2 %collective-permute-start.1 = (f32[840,128]{1,0:T(8,128)S(1)}, f32[840,128]{1,0:T(8,128)S(1)}, u32[]{:S(2)}, u32[]{:S(2)}) collective-permute-start(f32[840,128]{1,0:T(8,128)S(1)} %slice_bitcast_fusion), channel_id=1, source_target_pairs={{0,8},{1,9},{2,10},{3,11},{4,12},{5,13},{6,14},{7,15},{8,16},{9,17... | collective-permute-start | bytes 1290248 | tf_op jit(solution)/shard_map/ppermute | solution.py:688
  53.4 18.6 %collective-permute-start.2 = (f32[8,6,32,128]{3,2,1,0:T(8,128)S(1)}, f32[8,6,32,128]{3,2,1,0:T(8,128)S(1)}, u32[]{:S(2)}, u32[]{:S(2)}) collective-permute-start(f32[8,6,32,128]{3,2,1,0:T(8,128)S(1)} %get-tuple-element.111), channel_id=1, source_target_pairs={{0,7},{1,0},{2,1},{3,2},{4,3},{5,4},{6,5},{7,6},{8,15},{9,8},{10,9... | collective-permute-start | bytes 2359304 | tf_op jit(solution)/shard_map/ppermute | solution.py:688
  53.5 18.5 %collective-permute-start.3 = (f32[8,6,32,128]{3,2,1,0:T(8,128)S(1)}, f32[8,6,32,128]{3,2,1,0:T(8,128)S(1)}, u32[]{:S(2)}, u32[]{:S(2)}) collective-permute-start(f32[8,6,32,128]{3,2,1,0:T(8,128)S(1)} %get-tuple-element.110), channel_id=1, source_target_pairs={{0,1},{1,2},{2,3},{3,4},{4,5},{5,6},{6,7},{7,0},{8,9},{9,10},{10,1... | collective-permute-start | bytes 2359304 | tf_op jit(solution)/shard_map/ppermute | solution.py:688
  53.9 18.0 %collective-permute-start = (f32[768,128]{1,0:T(8,128)S(1)}, f32[768,128]{1,0:T(8,128)S(1)}, u32[]{:S(2)}, u32[]{:S(2)}) collective-permute-start(f32[768,128]{1,0:T(8,128)S(1)} %slice_bitcast_fusion.1), channel_id=1, source_target_pairs={{0,24},{1,25},{2,26},{3,27},{4,28},{5,29},{6,30},{7,31},{8,0},{9,1... | collective-permute-start | bytes 1179656 | tf_op jit(solution)/shard_map/ppermute | solution.py:688
  71.3 0.8 copy-start.3
  72.0 0.8 copy-start.16
  72.0 1.0 copy-start.7
  72.0 1.3 copy-start.10
  79.8 18.7 %collective-permute-start.6 = (f32[8,6,32,128]{3,2,1,0:T(8,128)}, f32[8,6,32,128]{3,2,1,0:T(8,128)S(1)}, u32[]{:S(2)}, u32[]{:S(2)}) collective-permute-start(f32[8,6,32,128]{3,2,1,0:T(8,128)} %get-tuple-element.57), channel_id=1, source_target_pairs={{0,7},{1,0},{2,1},{3,2},{4,3},{5,4},{6,5},{7,6},{8,15},{9,8},{10,9... | collective-permute-start | bytes 2359304 | tf_op jit(solution)/shard_map/ppermute | solution.py:688
  81.6 16.8 %collective-permute-start.7 = (f32[8,6,32,128]{3,2,1,0:T(8,128)}, f32[8,6,32,128]{3,2,1,0:T(8,128)S(1)}, u32[]{:S(2)}, u32[]{:S(2)}) collective-permute-start(f32[8,6,32,128]{3,2,1,0:T(8,128)} %get-tuple-element.58), channel_id=1, source_target_pairs={{0,1},{1,2},{2,3},{3,4},{4,5},{5,6},{6,7},{7,0},{8,9},{9,10},{10,1... | collective-permute-start | bytes 2359304 | tf_op jit(solution)/shard_map/ppermute | solution.py:688
  81.6 16.8 %collective-permute-start.4 = (f32[768,128]{1,0:T(8,128)}, f32[768,128]{1,0:T(8,128)S(1)}, u32[]{:S(2)}, u32[]{:S(2)}) collective-permute-start(f32[768,128]{1,0:T(8,128)} %get-tuple-element.55), channel_id=1, source_target_pairs={{0,24},{1,25},{2,26},{3,27},{4,28},{5,29},{6,30},{7,31},{8,0},{9,1... | collective-permute-start | bytes 1179656 | tf_op jit(solution)/shard_map/ppermute | solution.py:688
  83.3 15.1 %collective-permute-start.5 = (f32[768,128]{1,0:T(8,128)}, f32[768,128]{1,0:T(8,128)S(1)}, u32[]{:S(2)}, u32[]{:S(2)}) collective-permute-start(f32[768,128]{1,0:T(8,128)} %get-tuple-element.56), channel_id=1, source_target_pairs={{0,8},{1,9},{2,10},{3,11},{4,12},{5,13},{6,14},{7,15},{8,16},{9,17... | collective-permute-start | bytes 1179656 | tf_op jit(solution)/shard_map/ppermute | solution.py:688
  98.4 0.8 copy-start.15
  98.4 0.9 copy-start.18
  98.4 1.2 copy-start.8
  98.4 1.4 copy-start.11
  106.3 20.0 %collective-permute-start.10 = (f32[8,6,32,128]{3,2,1,0:T(8,128)}, f32[8,6,32,128]{3,2,1,0:T(8,128)S(1)}, u32[]{:S(2)}, u32[]{:S(2)}) collective-permute-start(f32[8,6,32,128]{3,2,1,0:T(8,128)} %get-tuple-element.63), channel_id=1, source_target_pairs={{0,7},{1,0},{2,1},{3,2},{4,3},{5,4},{6,5},{7,6},{8,15},{9,8},{10,9... | collective-permute-start | bytes 2359304 | tf_op jit(solution)/shard_map/ppermute | solution.py:688
  108.7 17.6 %collective-permute-start.11 = (f32[8,6,32,128]{3,2,1,0:T(8,128)}, f32[8,6,32,128]{3,2,1,0:T(8,128)S(1)}, u32[]{:S(2)}, u32[]{:S(2)}) collective-permute-start(f32[8,6,32,128]{3,2,1,0:T(8,128)} %get-tuple-element.64), channel_id=1, source_target_pairs={{0,1},{1,2},{2,3},{3,4},{4,5},{5,6},{6,7},{7,0},{8,9},{9,10},{10,1... | collective-permute-start | bytes 2359304 | tf_op jit(solution)/shard_map/ppermute | solution.py:688
  108.7 17.5 %collective-permute-start.8 = (f32[768,128]{1,0:T(8,128)}, f32[768,128]{1,0:T(8,128)S(1)}, u32[]{:S(2)}, u32[]{:S(2)}) collective-permute-start(f32[768,128]{1,0:T(8,128)} %get-tuple-element.61), channel_id=1, source_target_pairs={{0,24},{1,25},{2,26},{3,27},{4,28},{5,29},{6,30},{7,31},{8,0},{9,1... | collective-permute-start | bytes 1179656 | tf_op jit(solution)/shard_map/ppermute | solution.py:688
  111.6 14.6 %collective-permute-start.9 = (f32[768,128]{1,0:T(8,128)}, f32[768,128]{1,0:T(8,128)S(1)}, u32[]{:S(2)}, u32[]{:S(2)}) collective-permute-start(f32[768,128]{1,0:T(8,128)} %get-tuple-element.62), channel_id=1, source_target_pairs={{0,8},{1,9},{2,10},{3,11},{4,12},{5,13},{6,14},{7,15},{8,16},{9,17... | collective-permute-start | bytes 1179656 | tf_op jit(solution)/shard_map/ppermute | solution.py:688
  126.2 0.8 copy-start.14
  126.2 0.9 copy-start.17
  126.2 1.1 copy-start.6
  126.3 1.4 copy-start.9
  134.0 24.0 %collective-permute-start.17 = (f32[8,6,32,128]{3,2,1,0:T(8,128)}, f32[8,6,32,128]{3,2,1,0:T(8,128)S(1)}, u32[]{:S(2)}, u32[]{:S(2)}) collective-permute-start(f32[8,6,32,128]{3,2,1,0:T(8,128)} %get-tuple-element.72), channel_id=1, source_target_pairs={{0,7},{1,0},{2,1},{3,2},{4,3},{5,4},{6,5},{7,6},{8,15},{9,8},{10,9... | collective-permute-start | bytes 2359304 | tf_op jit(solution)/shard_map/ppermute | solution.py:688
  136.7 5.4 %copy-start.12 = (f32[768,128]{1,0:T(8,128)S(1)}, f32[768,128]{1,0:T(8,128)}, u32[]{:S(2)}) copy-start(f32[768,128]{1,0:T(8,128)} %get-tuple-element.71) | copy-start | bytes 1179652
  141.4 3.6 %collective-permute-start.12 = (f32[144,128]{1,0:T(8,128)}, f32[144,128]{1,0:T(8,128)S(1)}, u32[]{:S(2)}, u32[]{:S(2)}) collective-permute-start(f32[144,128]{1,0:T(8,128)} %get-tuple-element.68.gram_ref), channel_id=1, source_target_pairs={{0,1},{1,0},{2,3},{3,2},{4,5},{5,4},{6,7},{7,6},{8,9},{9,8},{10,11... | collective-permute-start | bytes 221192 | tf_op jit(solution)/shard_map/ppermute | solution.py:688
  142.1 15.9 %collective-permute-start.16 = (f32[768,128]{1,0:T(8,128)S(1)}, f32[768,128]{1,0:T(8,128)S(1)}, u32[]{:S(2)}, u32[]{:S(2)}) collective-permute-start(f32[768,128]{1,0:T(8,128)S(1)} %copy-done.12), channel_id=1, source_target_pairs={{0,24},{1,25},{2,26},{3,27},{4,28},{5,29},{6,30},{7,31},{8,0},{9,1... | collective-permute-start | bytes 1179656 | tf_op jit(solution)/shard_map/ppermute | solution.py:688
  145.9 12.0 %collective-permute-start.13 = (f32[144,128]{1,0:T(8,128)S(1)}, f32[144,128]{1,0:T(8,128)S(1)}, u32[]{:S(2)}, u32[]{:S(2)}) collective-permute-start(f32[144,128]{1,0:T(8,128)S(1)} %add.136), channel_id=1, source_target_pairs={{0,4},{1,5},{2,6},{3,7},{4,0},{5,1},{6,2},{7,3},{8,12},{9,13},{10,... | collective-permute-start | bytes 221192 | tf_op jit(solution)/shard_map/ppermute | solution.py:688
  146.0 11.9 %collective-permute-start.14 = (f32[144,128]{1,0:T(8,128)S(1)}, f32[144,128]{1,0:T(8,128)S(1)}, u32[]{:S(2)}, u32[]{:S(2)}) collective-permute-start(f32[144,128]{1,0:T(8,128)S(1)} %add.136), channel_id=1, source_target_pairs={{0,2},{1,3},{2,4},{3,5},{4,6},{5,7},{6,0},{7,1},{8,10},{9,11},{10,... | collective-permute-start | bytes 221192 | tf_op jit(solution)/shard_map/ppermute | solution.py:688
  147.3 10.7 %collective-permute-start.15 = (f32[144,128]{1,0:T(8,128)S(1)}, f32[144,128]{1,0:T(8,128)S(1)}, u32[]{:S(2)}, u32[]{:S(2)}) collective-permute-start(f32[144,128]{1,0:T(8,128)S(1)} %add.136), channel_id=1, source_target_pairs={{0,6},{1,7},{2,0},{3,1},{4,2},{5,3},{6,4},{7,5},{8,14},{9,15},{10,... | collective-permute-start | bytes 221192 | tf_op jit(solution)/shard_map/ppermute | solution.py:688
  158.0 0.8 copy-start.13
  158.0 4.0 %copy-start.5 = (f32[8,6,32,128]{3,2,1,0:T(8,128)}, f32[8,6,32,128]{3,2,1,0:T(8,128)S(1)}, u32[]{:S(2)}) copy-start(f32[8,6,32,128]{3,2,1,0:T(8,128)S(1)} %collective-permute-done.17.yu) | copy-start | bytes 2359300
  158.1 20.8 %collective-permute-start.18 = (f32[144,128]{1,0:T(8,128)S(1)}, f32[144,128]{1,0:T(8,128)S(1)}, u32[]{:S(2)}, u32[]{:S(2)}) collective-permute-start(f32[144,128]{1,0:T(8,128)S(1)} %add_add_fusion.1), channel_id=1, source_target_pairs={{0,16},{1,17},{2,18},{3,19},{4,20},{5,21},{6,22},{7,23},{8,24},{9,... | collective-permute-start | bytes 221192 | tf_op jit(solution)/shard_map/ppermute | solution.py:688
  158.8 20.1 %collective-permute-start.19 = (f32[144,128]{1,0:T(8,128)S(1)}, f32[144,128]{1,0:T(8,128)S(1)}, u32[]{:S(2)}, u32[]{:S(2)}) collective-permute-start(f32[144,128]{1,0:T(8,128)S(1)} %add_add_fusion.1), channel_id=1, source_target_pairs={{0,8},{1,9},{2,10},{3,11},{4,12},{5,13},{6,14},{7,15},{8,16},{9,17... | collective-permute-start | bytes 221192 | tf_op jit(solution)/shard_map/ppermute | solution.py:688
  159.8 19.1 %collective-permute-start.20 = (f32[144,128]{1,0:T(8,128)S(1)}, f32[144,128]{1,0:T(8,128)S(1)}, u32[]{:S(2)}, u32[]{:S(2)}) collective-permute-start(f32[144,128]{1,0:T(8,128)S(1)} %add_add_fusion.1), channel_id=1, source_target_pairs={{0,24},{1,25},{2,26},{3,27},{4,28},{5,29},{6,30},{7,31},{8,0},{9,1... | collective-permute-start | bytes 221192 | tf_op jit(solution)/shard_map/ppermute | solution.py:688
  162.0 46.7 %all-to-all-start.1 = ((f32[8,768,128]{2,1,0:T(8,128)}), f32[8,768,128]{2,1,0:T(8,128)S(1)}, u32[]{:S(2)}, u32[]{:S(2)}) async-start(f32[8,768,128]{2,1,0:T(8,128)} %get-tuple-element.76.here.above), calls=%async_computation.1 | async-start | bytes 6291456 | tf_op jit(solution)/shard_map/all_to_all | solution.py:692
  203.9 2.5 collective-permute-start.21
  208.7 1.6 copy-start.1
  210.4 23.4 %all-to-all-start.2 = ((f32[16,4,3200]{2,1,0:T(4,128)}), f32[16,4,3200]{2,1,0:T(4,128)S(1)}, u32[]{:S(2)}, u32[]{:S(2)}) async-start(f32[16,4,3200]{2,1,0:T(4,128)} %add.159), calls=%async_computation.2 | async-start | bytes 1638400 | tf_op jit(solution)/shard_map/all_to_all | solution.py:692
  216.1 18.5 %copy-start.19 = (s32[3]{0:T(128)S(1)}, s32[3]{0:T(128)}, u32[]{:S(2)}) copy-start(s32[3]{0:T(128)} %param.7) | copy-start | bytes 40
  216.1 18.6 %copy-start.2 = (f32[2,128,128]{2,1,0:T(8,128)S(1)}, f32[2,128,128]{2,1,0:T(8,128)}, u32[]{:S(2)}) copy-start(f32[2,128,128]{2,1,0:T(8,128)} %newton.1.z_ref) | copy-start | bytes 393220
  234.6 2.3 collective-permute-start.22
  239.1 20.4 %all-to-all-start.3 = ((f32[16,4,2560]{2,1,0:T(4,128)}), f32[16,4,2560]{2,1,0:T(4,128)S(1)}, u32[]{:S(2)}, u32[]{:S(2)}) async-start(f32[16,4,2560]{2,1,0:T(4,128)} %add.160), calls=%async_computation.3 | async-start | bytes 1310720 | tf_op jit(solution)/shard_map/all_to_all | solution.py:692
where the time goes:
time: 265 us; the launch traced here: 264 us
  Pallas kernels  142 us (54%)
  waiting for transfers between devices  54.6 us (21%)
  starting transfers between devices  48.7 us (18%)
  local copies, waits for them, and re-layouts  10.5 us (4%)
  other arithmetic  6.94 us (3%)
    all_to_all x4, waiting for transfers between devices, trade(): lax.all_to_all(value, 'sa', 0, 0, axis_index_groups=groups, tiled=True)  50 us
    pallas_call x3, Pallas kernels, interior(): pl.pallas_call(kernel, grid=(8 // STEP,), in_specs=in_specs, out_specs=ou...  43.7 us
    pallas_call x2, Pallas kernels, elementals(): pl.pallas_call(kernel, grid=(4,), in_specs=[pl.BlockSpec(memory_space=plt...  38.9 us
    ppermute x23, starting transfers between devices, move(): return lax.ppermute(value, 'sa', pairs)  27.2 us
    all_to_all x4, starting transfers between devices, trade(): lax.all_to_all(value, 'sa', 0, 0, axis_index_groups=groups, tiled=True)  21.5 us
    pallas_call x3, Pallas kernels, boundary(): pl.pallas_call(kernel, grid=(8 // FACE,), in_specs=[block, pl.BlockSpec((...  19.3 us
    pallas_call x1, Pallas kernels, carry_yz(): pl.pallas_call(kernel, grid=(8 // CARRY_YZ,), in_specs=[pl.BlockSpec((CAR...  13 us
    pallas_call x1, Pallas kernels, carry_x(): pl.pallas_call(kernel, grid=(8 // CARRY_X,), in_specs=[block, block, pl.B...  8.63 us
  transfers between devices with their start and end apart: 27, of which 4 were waited for; matrix products, arithmetic and copies ran while one was open for 2% of the time, Pallas kernels for 44%

commit v1 on v0

--- a/solution.py
+++ b/solution.py
@@ -17,12 +17,11 @@
 HIGHEST = lax.Precision.HIGHEST
 F32 = jnp.float32
 BF16 = jnp.bfloat16
-VMEM_LIMIT = 56 * 1024 * 1024
 LAY, STEP, FACE, GRAM, CARRY_X, CARRY_YZ, TURN = 4, 1, 4, 4, 2, 2, 4
 
 
-def params(**extra):
-    return pltpu.CompilerParams(vmem_limit_bytes=VMEM_LIMIT, **extra)
+def params(mebibytes):
+    return pltpu.CompilerParams(vmem_limit_bytes=mebibytes * 1024 * 1024)
 
 
 def link_of(rows, direction):
@@ -95,7 +94,7 @@
         ],
         out_specs=pl.BlockSpec((LAY, 840, 128), lambda q: (q, 0, 0)),
         out_shape=jax.ShapeDtypeStruct((8, 840, 128), F32),
-        compiler_params=params(),
+        compiler_params=params(16),
         cost_estimate=pl.CostEstimate(flops=3_000_000_000, bytes_accessed=7_000_000, transcendentals=0),
         name="lay_out",
     )(field, links)
@@ -198,7 +197,7 @@
             pltpu.VMEM((6, 32, 128), F32),
             pltpu.VMEM((6, 128, 128), F32),
         ],
-        compiler_params=params(),
+        compiler_params=params(12),
         cost_estimate=pl.CostEstimate(flops=12_000_000_000, bytes_accessed=12_000_000, transcendentals=0),
         name=name,
     )(*operands)
@@ -282,7 +281,7 @@
             jax.ShapeDtypeStruct((768, 128), F32),
         ),
         scratch_shapes=[pltpu.VMEM((128, 128), F32)],
-        compiler_params=params(),
+        compiler_params=params(20),
         cost_estimate=pl.CostEstimate(flops=6_000_000_000, bytes_accessed=9_000_000, transcendentals=0),
         name=name,
     )(partial, links, z_up, z_down, y_up, y_down, z_links)
@@ -340,7 +339,7 @@
         out_specs=(pl.BlockSpec((144, 128), lambda z: (0, 0)), pl.BlockSpec((GRAM, 768, 128), lambda z: (z, 0, 0))),
         out_shape=(jax.ShapeDtypeStruct((144, 128), F32), jax.ShapeDtypeStruct((8, 768, 128), F32)),
         scratch_shapes=[pltpu.VMEM((256, 256), F32)],
-        compiler_params=params(),
+        compiler_params=params(28),
         cost_estimate=pl.CostEstimate(flops=4_000_000_000, bytes_accessed=3_000_000, transcendentals=0),
         name="gram",
     )(u, first_norm, second_norm)
@@ -407,7 +406,7 @@
             pltpu.VMEM((1, 6, 128, 128), F32),
             pltpu.VMEM((256, 256), F32),
         ],
-        compiler_params=params(),
+        compiler_params=params(20),
         cost_estimate=pl.CostEstimate(flops=7_000_000_000, bytes_accessed=8_000_000, transcendentals=0),
         name="carry_x",
     )(u, turned, links)
@@ -473,7 +472,7 @@
         out_specs=(pl.BlockSpec((CARRY_YZ, 1152, 512), lambda z: (z, 0, 0)), pl.BlockSpec((128, 128), lambda z: (0, 0))),
         out_shape=(jax.ShapeDtypeStruct((8, 1152, 512), BF16), jax.ShapeDtypeStruct((128, 128), F32)),
         scratch_shapes=[pltpu.VMEM((2, 6, 128, 128), F32), pltpu.VMEM((256, 256), F32)],
-        compiler_params=params(),
+        compiler_params=params(24),
         cost_estimate=pl.CostEstimate(flops=12_000_000_000, bytes_accessed=16_000_000, transcendentals=0),
         name="carry_yz",
     )(u, turned, u, links, z_up, y_up, x_hops, packed_gram)
@@ -563,7 +562,7 @@
             pltpu.VMEM((count * 256, 2304), BF16),
             pltpu.VMEM((count * 256, 768), F32),
         ],
-        compiler_params=params(),
+        compiler_params=params(40),
         cost_estimate=pl.CostEstimate(flops=5_500_000_000 * count, bytes_accessed=16_000_000, transcendentals=0),
         name=name,
     )(core, z, turned_u, right_x, right_yz, phases, *([] if extra is None else [extra]))
@@ -614,7 +613,7 @@
     return pl.pallas_call(
         kernel,
         out_shape=jax.ShapeDtypeStruct((2, 128, 128), F32),
-        compiler_params=params(),
+        compiler_params=params(12),
         cost_estimate=pl.CostEstimate(flops=5_000_000_000, bytes_accessed=300_000, transcendentals=0),
         name="newton",
     )(total)
@@ -632,7 +631,7 @@
     return pl.pallas_call(
         kernel,
         out_shape=jax.ShapeDtypeStruct((2, 128, 128), F32),
-        compiler_params=params(),
+        compiler_params=params(12),
         cost_estimate=pl.CostEstimate(flops=3_000_000_000, bytes_accessed=300_000, transcendentals=0),
         name="rayleigh",
     )(total, z)
@@ -661,7 +660,7 @@
         ],
         out_specs=pl.BlockSpec((6, 128 * TURN, 128), lambda i: (0, i, 0)),
         out_shape=jax.ShapeDtypeStruct((6, 1024, 128), F32),
-        compiler_params=params(),
+        compiler_params=params(24),
         cost_estimate=pl.CostEstimate(flops=5_000_000_000, bytes_accessed=7_000_000, transcendentals=0),
         name="rotate",
     )(z, blocks)

time: 265 us -> 259 us (0.977)
  Pallas kernels: 142 us -> 111 us
  local copies, waits for them, and re-layouts: 10.5 us -> 31.6 us
    unnamed x42 -> x52, local copies, waits for them, and re-layouts: 6.96 us -> 29.4 us
    pallas_call x3, Pallas kernels: 19.3 us -> 9.71 us  [boundary(): pl.pallas_call(kernel, grid=(8 // FACE,), in_specs=[block, pl.BlockSpec((...]
    pallas_call x3, Pallas kernels: 43.7 us -> 38.6 us  [interior(): pl.pallas_call(kernel, grid=(8 // STEP,), in_specs=in_specs, out_specs=ou...]
    pallas_call x2, Pallas kernels: 38.9 us -> 34 us  [elementals(): pl.pallas_call(kernel, grid=(4,), in_specs=[pl.BlockSpec(memory_space=plt...]
  transfers between devices with their start and end apart: 27 -> 27, of which waited for: 4 -> 4; matrix products, arithmetic and copies ran while one was open for 2% -> 2% of each run, Pallas kernels for 44% -> 38%
where the time goes in v1:
time: 259 us; the launch traced here: 258 us
  Pallas kernels  111 us (43%)
  waiting for transfers between devices  55.3 us (21%)
  starting transfers between devices  49.5 us (19%)
  local copies, waits for them, and re-layouts  31.6 us (12%)
  other arithmetic  8.52 us (3%)
    all_to_all x4, waiting for transfers between devices, trade(): lax.all_to_all(value, 'sa', 0, 0, axis_index_groups=groups, tiled=True)  51.4 us
    pallas_call x3, Pallas kernels, interior(): pl.pallas_call(kernel, grid=(8 // STEP,), in_specs=in_specs, out_specs=ou...  38.6 us
    pallas_call x2, Pallas kernels, elementals(): pl.pallas_call(kernel, grid=(4,), in_specs=[pl.BlockSpec(memory_space=plt...  34 us
    unnamed x52, local copies, waits for them, and re-layouts  29.4 us
    ppermute x23, starting transfers between devices, move(): return lax.ppermute(value, 'sa', pairs)  27.4 us
    all_to_all x4, starting transfers between devices, trade(): lax.all_to_all(value, 'sa', 0, 0, axis_index_groups=groups, tiled=True)  22.1 us
    pallas_call x1, Pallas kernels, carry_yz(): pl.pallas_call(kernel, grid=(8 // CARRY_YZ,), in_specs=[pl.BlockSpec((CAR...  10.6 us
    pallas_call x3, Pallas kernels, boundary(): pl.pallas_call(kernel, grid=(8 // FACE,), in_specs=[block, pl.BlockSpec((...  9.71 us
  transfers between devices with their start and end apart: 27, of which 4 were waited for; matrix products, arithmetic and copies ran while one was open for 2% of the time, Pallas kernels for 38%

profile of v1, /device:TPU:0, one launch (start us, length us, event | category | flops | bytes accessed | tf_op | source)
XLA Modules:
  0.0 258.0 jit_solution(11880559651489520375)
XLA Ops:
  0.6 1.9 copy-done.2
  2.5 1.2 copy-done.3
  3.7 1.5 lay_out.1
  5.2 1.7 copy-done
  6.9 4.7 %all-to-all-start = ((f32[8,840,128]{2,1,0:T(8,128)}), f32[8,840,128]{2,1,0:T(8,128)S(1)}, u32[]{:S(2)}, u32[]{:S(2)}) async-start(f32[8,840,128]{2,1,0:T(8,128)} %copy-done), calls=%async_computation | async-start | bytes 6881280 | tf_op jit(solution)/shard_map/all_to_all | solution.py:691
  12.2 41.0 %all-to-all-done.refs_0_.refs_1_.refs_3_ = f32[8,840,128]{2,1,0:T(8,128)S(1)} async-done(((f32[8,840,128]{2,1,0:T(8,128)}), f32[8,840,128]{2,1,0:T(8,128)S(1)}, u32[]{:S(2)}, u32[]{:S(2)}) %all-to-all-start) | async-done | bytes 3440672 | tf_op jit(solution)/shard_map/all_to_all | solution.py:691
  53.2 2.0 collective-permute-start.1
  56.1 2.2 collective-permute-start
  58.3 12.9 %interior_0.1 = (f32[8,768,128]{2,1,0:T(8,128)S(1)}, f32[8,128]{1,0:T(8,128)}, f32[8,128,128]{2,1,0:T(8,128)S(1)}) custom-call(f32[8,840,128]{2,1,0:T(8,128)S(1)} %all-to-all-done.refs_0_.refs_1_.refs_3_, f32[8,840,128]{2,1,0:T(8,128)S(1)} %all-to-all-done.refs_0_.refs_1_.refs_3_), custom_call_target="tpu_custom_call" | custom-call | flops 12000000000 | bytes 12000000 | tf_op jit(solution)/shard_map/interior_0/pallas_call | solution.py:188
  71.3 2.8 %boundary_0.1 = (f32[8,768,128]{2,1,0:T(8,128)S(1)}, f32[8,6,32,128]{3,2,1,0:T(8,128)S(1)}, f32[8,6,32,128]{3,2,1,0:T(8,128)S(1)}, f32[768,128]{1,0:T(8,128)S(1)}, f32[768,128]{1,0:T(8,128)S(1)}) custom-call(f32[8,768,128]{2,1,0:T(8,128)S(1)} %get-tuple-element.51.part, f32[8,128,128]{2,1,0:T(8,128)S(1)} %get-tuple-element.52.link_ref.refs_2_, ...), custom_call_target="tpu_custom_call" | custom-call | flops 6000000000 | bytes 9000000 | tf_op jit(solution)/shard_map/boundary_0/pallas_call | solution.py:263
  74.1 2.6 %collective-permute-start.6 = (f32[8,6,32,128]{3,2,1,0:T(8,128)S(1)}, f32[8,6,32,128]{3,2,1,0:T(8,128)S(1)}, u32[]{:S(2)}, u32[]{:S(2)}) collective-permute-start(f32[8,6,32,128]{3,2,1,0:T(8,128)S(1)} %get-tuple-element.57), channel_id=1, source_target_pairs={{0,7},{1,0},{2,1},{3,2},{4,3},{5,4},{6,5},{7,6},{8,15},{9,8},{10,9... | collective-permute-start | bytes 2359304 | tf_op jit(solution)/shard_map/ppermute | solution.py:687
  76.7 1.7 collective-permute-start.4
  78.7 12.9 %interior_1.1 = (f32[8,768,128]{2,1,0:T(8,128)S(1)}, f32[8,128]{1,0:T(8,128)S(1)}) custom-call(f32[8,768,128]{2,1,0:T(8,128)S(1)} %get-tuple-element.53.refs_0_.refs_1_.refs_3_, f32[8,768,128]{2,1,0:T(8,128)S(1)} %get-tuple-element.53.refs_0_.refs_1_.refs_3_, f32[8,128,128]{2,1,0:T(8,128)S(1)} %get-tuple-element.52.link_ref.refs_2_, ...), custom_call_target="tpu_custom_call" | custom-call | flops 12000000000 | bytes 12000000 | tf_op jit(solution)/shard_map/interior_1/pallas_call | solution.py:188
  91.7 2.8 %boundary_1.1 = (f32[8,768,128]{2,1,0:T(8,128)S(1)}, f32[8,6,32,128]{3,2,1,0:T(8,128)S(1)}, f32[8,6,32,128]{3,2,1,0:T(8,128)S(1)}, f32[768,128]{1,0:T(8,128)S(1)}, f32[768,128]{1,0:T(8,128)S(1)}) custom-call(f32[8,768,128]{2,1,0:T(8,128)S(1)} %get-tuple-element.54.part, f32[8,128,128]{2,1,0:T(8,128)S(1)} %get-tuple-element.52.link_ref.refs_2_, ...), custom_call_target="tpu_custom_call" | custom-call | flops 6000000000 | bytes 9000000 | tf_op jit(solution)/shard_map/boundary_1/pallas_call | solution.py:263
  94.4 2.4 collective-permute-start.10
  96.8 2.9 %collective-permute-start.8 = (f32[768,128]{1,0:T(8,128)S(1)}, f32[768,128]{1,0:T(8,128)S(1)}, u32[]{:S(2)}, u32[]{:S(2)}) collective-permute-start(f32[768,128]{1,0:T(8,128)S(1)} %get-tuple-element.61), channel_id=1, source_target_pairs={{0,24},{1,25},{2,26},{3,27},{4,28},{5,29},{6,30},{7,31},{8,0},{9,1... | collective-permute-start | bytes 1179656 | tf_op jit(solution)/shard_map/ppermute | solution.py:687
  99.8 12.7 %interior_2.1 = (f32[8,768,128]{2,1,0:T(8,128)S(1)}, f32[8,128]{1,0:T(8,128)S(1)}) custom-call(f32[8,768,128]{2,1,0:T(8,128)S(1)} %get-tuple-element.59.refs_0_.refs_1_, f32[8,768,128]{2,1,0:T(8,128)S(1)} %get-tuple-element.59.refs_0_.refs_1_, f32[8,128,128]{2,1,0:T(8,128)S(1)} %get-tuple-element.52.link_ref.refs_2_, ...), custom_call_target="tpu_custom_call" | custom-call | flops 12000000000 | bytes 12000000 | tf_op jit(solution)/shard_map/interior_2/pallas_call | solution.py:188
  112.6 4.2 %boundary_2.1 = (f32[8,768,128]{2,1,0:T(8,128)}, f32[8,6,32,128]{3,2,1,0:T(8,128)S(1)}, f32[8,6,32,128]{3,2,1,0:T(8,128)}, f32[768,128]{1,0:T(8,128)S(1)}, f32[768,128]{1,0:T(8,128)}) custom-call(f32[8,768,128]{2,1,0:T(8,128)S(1)} %get-tuple-element.60.part, f32[8,128,128]{2,1,0:T(8,128)S(1)} %get-tuple-element.52.link_ref.refs_2_, ...), custom_call_target="tpu_custom_call" | custom-call | flops 6000000000 | bytes 9000000 | tf_op jit(solution)/shard_map/boundary_2/pallas_call | solution.py:263
  116.8 2.7 %collective-permute-start.17 = (f32[8,6,32,128]{3,2,1,0:T(8,128)S(1)}, f32[8,6,32,128]{3,2,1,0:T(8,128)S(1)}, u32[]{:S(2)}, u32[]{:S(2)}) collective-permute-start(f32[8,6,32,128]{3,2,1,0:T(8,128)S(1)} %get-tuple-element.72), channel_id=1, source_target_pairs={{0,7},{1,0},{2,1},{3,2},{4,3},{5,4},{6,5},{7,6},{8,15},{9,8},{10,9... | collective-permute-start | bytes 2359304 | tf_op jit(solution)/shard_map/ppermute | solution.py:687
  119.4 3.9 %gram.1 = (f32[144,128]{1,0:T(8,128)S(1)}, f32[8,768,128]{2,1,0:T(8,128)S(1)}) custom-call(f32[8,768,128]{2,1,0:T(8,128)} %get-tuple-element.76.here.above, f32[8,128]{1,0:T(8,128)S(1)} %get-tuple-element.66.n1, f32[8,128]{1,0:T(8,128)S(1)} %get-tuple-element.67.n2), custom_call_target="tpu_custom_call" | custom-call | flops 4000000000 | bytes 3000000 | tf_op jit(solution)/shard_map/gram/pallas_call | solution.py:335
  123.4 1.6 copy-done.9
  125.0 3.0 %collective-permute-start.16 = (f32[768,128]{1,0:T(8,128)S(1)}, f32[768,128]{1,0:T(8,128)S(1)}, u32[]{:S(2)}, u32[]{:S(2)}) collective-permute-start(f32[768,128]{1,0:T(8,128)S(1)} %get-tuple-element.71), channel_id=1, source_target_pairs={{0,24},{1,25},{2,26},{3,27},{4,28},{5,29},{6,30},{7,31},{8,0},{9,1... | collective-permute-start | bytes 1179656 | tf_op jit(solution)/shard_map/ppermute | solution.py:687
  128.2 1.3 collective-permute-start.14
  129.4 2.1 collective-permute-start.15
  131.5 1.9 copy-done.10
  133.4 6.8 %carry_x.1 = (bf16[8,1152,256]{2,1,0:T(8,128)(2,1)S(1)}, f32[256,256]{1,0:T(8,128)S(1)}) custom-call(f32[8,768,128]{2,1,0:T(8,128)} %get-tuple-element.76.here.above, f32[8,768,128]{2,1,0:T(8,128)S(1)} %copy-done.10, f32[8,128,128]{2,1,0:T(8,128)S(1)} %copy-done.19), custom_call_target="tpu_custom_call" | custom-call | flops 7000000000 | bytes 8000000 | tf_op jit(solution)/shard_map/carry_x/pallas_call | solution.py:398
  140.2 2.2 copy-done.14
  142.4 0.7 copy-done.21
  143.1 0.7 copy-done.7
  143.9 0.9 copy-done.4
  144.9 2.0 collective-permute-start.19
  146.9 1.3 collective-permute-start.20
  148.2 3.9 %all-to-all-start.1 = ((f32[8,768,128]{2,1,0:T(8,128)}), f32[8,768,128]{2,1,0:T(8,128)S(1)}, u32[]{:S(2)}, u32[]{:S(2)}) async-start(f32[8,768,128]{2,1,0:T(8,128)} %get-tuple-element.76.here.above), calls=%async_computation.1 | async-start | bytes 6291456 | tf_op jit(solution)/shard_map/all_to_all | solution.py:691
  152.1 1.1 copy-done.5
  153.2 1.0 copy-done.8
  154.2 1.9 copy-done.11
  156.1 1.0 copy-done.20
  157.1 0.9 copy-done.22
  158.1 10.6 %carry_yz.1 = (bf16[8,1152,512]{2,1,0:T(8,128)(2,1)S(1)}, f32[128,128]{1,0:T(8,128)S(1)}) custom-call(f32[8,768,128]{2,1,0:T(8,128)} %get-tuple-element.76.here.above, f32[8,768,128]{2,1,0:T(8,128)S(1)} %copy-done.11, f32[8,768,128]{2,1,0:T(8,128)} %get-tuple-element.76.here.above, f32[8,128,128]{2,1,0:T(8,128)S(1)} %copy-done.20, f32[768,128]{1,0:T(8,128)S(1)} %copy-done.8, ...), custom_call_target="tpu_custom_call" | custom-call | flops 12000000000 | bytes 16000000 | tf_op jit(solution)/shard_map/carry_yz/pallas_call | solution.py:459
  168.7 1.1 add_add_fusion.ref
  169.9 1.6 newton.1.z_ref
  171.5 1.5 copy-done.17
  173.0 1.0 copy-done.12
  174.0 1.4 copy-done.15
  175.4 19.0 %elementals_0.1 = (f32[16,4,3200]{2,1,0:T(4,128)S(1)}, f32[16,4,3200]{2,1,0:T(4,128)S(1)}) custom-call(s32[1]{0:T(128)} %bitcast.5.core_ref, f32[2,128,128]{2,1,0:T(8,128)S(1)} %newton.1.z_ref, f32[8,768,128]{2,1,0:T(8,128)S(1)} %copy-done.12, bf16[8,1152,256]{2,1,0:T(8,128)(2,1)S(1)} %copy-done.15, bf16[8,1152,512]{2,1,0:T(8,128)(2,1)} %copy-done.17, ...), custom_call_target="tpu_custom_call" | custom-call | flops 22000001024 | bytes 16000000 | tf_op jit(solution)/shard_map/elementals_0/pallas_call | solution.py:547
  194.7 2.2 collective-permute-done.21
  196.8 1.1 add.159
  197.9 6.3 %all-to-all-start.2 = ((f32[16,4,3200]{2,1,0:T(4,128)}), f32[16,4,3200]{2,1,0:T(4,128)}, u32[]{:S(2)}, u32[]{:S(2)}) async-start(f32[16,4,3200]{2,1,0:T(4,128)} %add.159), calls=%async_computation.2 | async-start | bytes 1638400 | tf_op jit(solution)/shard_map/all_to_all | solution.py:691
  204.3 1.9 copy-done.13
  206.2 2.3 copy-done.16
  208.5 14.9 %elementals_1.1 = (f32[16,4,2560]{2,1,0:T(4,128)S(1)}, f32[16,4,2560]{2,1,0:T(4,128)S(1)}) custom-call(s32[1]{0:T(128)} %bitcast.5.core_ref, f32[2,128,128]{2,1,0:T(8,128)S(1)} %newton.1.z_ref, f32[8,768,128]{2,1,0:T(8,128)S(1)} %copy-done.13, bf16[8,1152,256]{2,1,0:T(8,128)(2,1)S(1)} %copy-done.16, bf16[8,1152,512]{2,1,0:T(8,128)(2,1)} %copy-done.17, ...), custom_call_target="tpu_custom_call" | custom-call | flops 16499999744 | bytes 16000000 | tf_op jit(solution)/shard_map/elementals_1/pallas_call | solution.py:547
  223.5 0.8 copy-done.1
  224.3 0.8 copy-done.6
  225.2 1.3 reduce_sum.27
  227.8 1.7 collective-permute-done.22
  229.5 2.3 add.160
  231.8 7.2 %all-to-all-start.3 = ((f32[16,4,2560]{2,1,0:T(4,128)}), f32[16,4,2560]{2,1,0:T(4,128)}, u32[]{:S(2)}, u32[]{:S(2)}) async-start(f32[16,4,2560]{2,1,0:T(4,128)} %add.160), calls=%async_computation.3 | async-start | bytes 1310720 | tf_op jit(solution)/shard_map/all_to_all | solution.py:691
  239.1 2.7 %rotate.1 = f32[6,1024,128]{2,1,0:T(8,128)} custom-call(f32[2,128,128]{2,1,0:T(8,128)S(1)} %newton.1.z_ref, f32[8,768,128]{2,1,0:T(8,128)S(1)} %all-to-all-done.1.ref), custom_call_target="tpu_custom_call" | custom-call | flops 5000000000 | bytes 7000000 | tf_op jit(solution)/shard_map/rotate/pallas_call | solution.py:654
  241.9 10.5 %all-to-all-done.3 = f32[16,4,2560]{2,1,0:T(4,128)} async-done(((f32[16,4,2560]{2,1,0:T(4,128)}), f32[16,4,2560]{2,1,0:T(4,128)}, u32[]{:S(2)}, u32[]{:S(2)}) %all-to-all-start.3) | async-done | bytes 655392 | tf_op jit(solution)/shard_map/all_to_all | solution.py:691
  252.3 1.1 slice_reduce_fusion
  253.8 1.2 convolution_multiply_fusion
  255.2 0.7 copy.16
  255.9 0.8 select_bitcast_fusion.1
  256.7 1.3 rayleigh.1
  (99 shorter events, 4.4 us)
Async XLA Ops:
  0.6 1.9 copy-start.2
  2.5 1.2 copy-start.3
  5.2 1.7 copy-start
  6.9 4.7 %copy-start.23 = (s32[7,3]{0,1:T(4,128)S(1)}, s32[7,3]{0,1:T(4,128)}, u32[]{:S(2)}) copy-start(s32[7,3]{0,1:T(4,128)} %param.6) | copy-start | bytes 256
  6.9 46.3 %all-to-all-start = ((f32[8,840,128]{2,1,0:T(8,128)}), f32[8,840,128]{2,1,0:T(8,128)S(1)}, u32[]{:S(2)}, u32[]{:S(2)}) async-start(f32[8,840,128]{2,1,0:T(8,128)} %copy-done), calls=%async_computation | async-start | bytes 6881280 | tf_op jit(solution)/shard_map/all_to_all | solution.py:691
  53.2 18.1 %collective-permute-start.1 = (f32[840,128]{1,0:T(8,128)S(1)}, f32[840,128]{1,0:T(8,128)S(1)}, u32[]{:S(2)}, u32[]{:S(2)}) collective-permute-start(f32[840,128]{1,0:T(8,128)S(1)} %slice_bitcast_fusion), channel_id=1, source_target_pairs={{0,8},{1,9},{2,10},{3,11},{4,12},{5,13},{6,14},{7,15},{8,16},{9,17... | collective-permute-start | bytes 1290248 | tf_op jit(solution)/shard_map/ppermute | solution.py:687
  55.6 15.7 %collective-permute-start.2 = (f32[8,6,32,128]{3,2,1,0:T(8,128)S(1)}, f32[8,6,32,128]{3,2,1,0:T(8,128)S(1)}, u32[]{:S(2)}, u32[]{:S(2)}) collective-permute-start(f32[8,6,32,128]{3,2,1,0:T(8,128)S(1)} %get-tuple-element.111), channel_id=1, source_target_pairs={{0,7},{1,0},{2,1},{3,2},{4,3},{5,4},{6,5},{7,6},{8,15},{9,8},{10,9... | collective-permute-start | bytes 2359304 | tf_op jit(solution)/shard_map/ppermute | solution.py:687
  55.7 15.6 %collective-permute-start.3 = (f32[8,6,32,128]{3,2,1,0:T(8,128)S(1)}, f32[8,6,32,128]{3,2,1,0:T(8,128)S(1)}, u32[]{:S(2)}, u32[]{:S(2)}) collective-permute-start(f32[8,6,32,128]{3,2,1,0:T(8,128)S(1)} %get-tuple-element.110), channel_id=1, source_target_pairs={{0,1},{1,2},{2,3},{3,4},{4,5},{5,6},{6,7},{7,0},{8,9},{9,10},{10,1... | collective-permute-start | bytes 2359304 | tf_op jit(solution)/shard_map/ppermute | solution.py:687
  56.1 15.2 %collective-permute-start = (f32[768,128]{1,0:T(8,128)S(1)}, f32[768,128]{1,0:T(8,128)S(1)}, u32[]{:S(2)}, u32[]{:S(2)}) collective-permute-start(f32[768,128]{1,0:T(8,128)S(1)} %slice_bitcast_fusion.1), channel_id=1, source_target_pairs={{0,24},{1,25},{2,26},{3,27},{4,28},{5,29},{6,30},{7,31},{8,0},{9,1... | collective-permute-start | bytes 1179656 | tf_op jit(solution)/shard_map/ppermute | solution.py:687
  71.3 41.3 %copy-start.18 = (f32[8,128,128]{2,1,0:T(8,128)}, f32[8,128,128]{2,1,0:T(8,128)S(1)}, u32[]{:S(2)}) copy-start(f32[8,128,128]{2,1,0:T(8,128)S(1)} %get-tuple-element.52.link_ref.refs_2_) | copy-start | bytes 1572868
  74.1 17.5 %collective-permute-start.6 = (f32[8,6,32,128]{3,2,1,0:T(8,128)S(1)}, f32[8,6,32,128]{3,2,1,0:T(8,128)S(1)}, u32[]{:S(2)}, u32[]{:S(2)}) collective-permute-start(f32[8,6,32,128]{3,2,1,0:T(8,128)S(1)} %get-tuple-element.57), channel_id=1, source_target_pairs={{0,7},{1,0},{2,1},{3,2},{4,3},{5,4},{6,5},{7,6},{8,15},{9,8},{10,9... | collective-permute-start | bytes 2359304 | tf_op jit(solution)/shard_map/ppermute | solution.py:687
  76.7 15.0 %collective-permute-start.7 = (f32[8,6,32,128]{3,2,1,0:T(8,128)S(1)}, f32[8,6,32,128]{3,2,1,0:T(8,128)S(1)}, u32[]{:S(2)}, u32[]{:S(2)}) collective-permute-start(f32[8,6,32,128]{3,2,1,0:T(8,128)S(1)} %get-tuple-element.58), channel_id=1, source_target_pairs={{0,1},{1,2},{2,3},{3,4},{4,5},{5,6},{6,7},{7,0},{8,9},{9,10},{10,1... | collective-permute-start | bytes 2359304 | tf_op jit(solution)/shard_map/ppermute | solution.py:687
  76.7 14.9 %collective-permute-start.4 = (f32[768,128]{1,0:T(8,128)S(1)}, f32[768,128]{1,0:T(8,128)S(1)}, u32[]{:S(2)}, u32[]{:S(2)}) collective-permute-start(f32[768,128]{1,0:T(8,128)S(1)} %get-tuple-element.55), channel_id=1, source_target_pairs={{0,24},{1,25},{2,26},{3,27},{4,28},{5,29},{6,30},{7,31},{8,0},{9,1... | collective-permute-start | bytes 1179656 | tf_op jit(solution)/shard_map/ppermute | solution.py:687
  78.4 13.2 %collective-permute-start.5 = (f32[768,128]{1,0:T(8,128)S(1)}, f32[768,128]{1,0:T(8,128)S(1)}, u32[]{:S(2)}, u32[]{:S(2)}) collective-permute-start(f32[768,128]{1,0:T(8,128)S(1)} %get-tuple-element.56), channel_id=1, source_target_pairs={{0,8},{1,9},{2,10},{3,11},{4,12},{5,13},{6,14},{7,15},{8,16},{9,17... | collective-permute-start | bytes 1179656 | tf_op jit(solution)/shard_map/ppermute | solution.py:687
  94.4 18.1 %collective-permute-start.10 = (f32[8,6,32,128]{3,2,1,0:T(8,128)S(1)}, f32[8,6,32,128]{3,2,1,0:T(8,128)S(1)}, u32[]{:S(2)}, u32[]{:S(2)}) collective-permute-start(f32[8,6,32,128]{3,2,1,0:T(8,128)S(1)} %get-tuple-element.63), channel_id=1, source_target_pairs={{0,7},{1,0},{2,1},{3,2},{4,3},{5,4},{6,5},{7,6},{8,15},{9,8},{10,9... | collective-permute-start | bytes 2359304 | tf_op jit(solution)/shard_map/ppermute | solution.py:687
  96.8 15.7 %collective-permute-start.11 = (f32[8,6,32,128]{3,2,1,0:T(8,128)S(1)}, f32[8,6,32,128]{3,2,1,0:T(8,128)S(1)}, u32[]{:S(2)}, u32[]{:S(2)}) collective-permute-start(f32[8,6,32,128]{3,2,1,0:T(8,128)S(1)} %get-tuple-element.64), channel_id=1, source_target_pairs={{0,1},{1,2},{2,3},{3,4},{4,5},{5,6},{6,7},{7,0},{8,9},{9,10},{10,1... | collective-permute-start | bytes 2359304 | tf_op jit(solution)/shard_map/ppermute | solution.py:687
  96.8 15.7 %collective-permute-start.8 = (f32[768,128]{1,0:T(8,128)S(1)}, f32[768,128]{1,0:T(8,128)S(1)}, u32[]{:S(2)}, u32[]{:S(2)}) collective-permute-start(f32[768,128]{1,0:T(8,128)S(1)} %get-tuple-element.61), channel_id=1, source_target_pairs={{0,24},{1,25},{2,26},{3,27},{4,28},{5,29},{6,30},{7,31},{8,0},{9,1... | collective-permute-start | bytes 1179656 | tf_op jit(solution)/shard_map/ppermute | solution.py:687
  99.8 12.8 %collective-permute-start.9 = (f32[768,128]{1,0:T(8,128)S(1)}, f32[768,128]{1,0:T(8,128)S(1)}, u32[]{:S(2)}, u32[]{:S(2)}) collective-permute-start(f32[768,128]{1,0:T(8,128)S(1)} %get-tuple-element.62), channel_id=1, source_target_pairs={{0,8},{1,9},{2,10},{3,11},{4,12},{5,13},{6,14},{7,15},{8,16},{9,17... | collective-permute-start | bytes 1179656 | tf_op jit(solution)/shard_map/ppermute | solution.py:687
  116.8 27.1 %collective-permute-start.17 = (f32[8,6,32,128]{3,2,1,0:T(8,128)S(1)}, f32[8,6,32,128]{3,2,1,0:T(8,128)S(1)}, u32[]{:S(2)}, u32[]{:S(2)}) collective-permute-start(f32[8,6,32,128]{3,2,1,0:T(8,128)S(1)} %get-tuple-element.72), channel_id=1, source_target_pairs={{0,7},{1,0},{2,1},{3,2},{4,3},{5,4},{6,5},{7,6},{8,15},{9,8},{10,9... | collective-permute-start | bytes 2359304 | tf_op jit(solution)/shard_map/ppermute | solution.py:687
  119.4 12.0 %copy-start.19 = (f32[8,128,128]{2,1,0:T(8,128)S(1)}, f32[8,128,128]{2,1,0:T(8,128)}, u32[]{:S(2)}) copy-start(f32[8,128,128]{2,1,0:T(8,128)} %copy-done.18) | copy-start | bytes 1572868
  123.3 1.6 copy-start.9
  125.0 3.1 %collective-permute-start.12 = (f32[144,128]{1,0:T(8,128)S(1)}, f32[144,128]{1,0:T(8,128)S(1)}, u32[]{:S(2)}, u32[]{:S(2)}) collective-permute-start(f32[144,128]{1,0:T(8,128)S(1)} %get-tuple-element.68.gram_ref), channel_id=1, source_target_pairs={{0,1},{1,0},{2,3},{3,2},{4,5},{5,4},{6,7},{7,6},{8,9},{9,8},{10,11... | collective-permute-start | bytes 221192 | tf_op jit(solution)/shard_map/ppermute | solution.py:687
  125.0 18.0 %collective-permute-start.16 = (f32[768,128]{1,0:T(8,128)S(1)}, f32[768,128]{1,0:T(8,128)S(1)}, u32[]{:S(2)}, u32[]{:S(2)}) collective-permute-start(f32[768,128]{1,0:T(8,128)S(1)} %get-tuple-element.71), channel_id=1, source_target_pairs={{0,24},{1,25},{2,26},{3,27},{4,28},{5,29},{6,30},{7,31},{8,0},{9,1... | collective-permute-start | bytes 1179656 | tf_op jit(solution)/shard_map/ppermute | solution.py:687
  128.1 15.0 %collective-permute-start.13 = (f32[144,128]{1,0:T(8,128)S(1)}, f32[144,128]{1,0:T(8,128)S(1)}, u32[]{:S(2)}, u32[]{:S(2)}) collective-permute-start(f32[144,128]{1,0:T(8,128)S(1)} %add.136), channel_id=1, source_target_pairs={{0,4},{1,5},{2,6},{3,7},{4,0},{5,1},{6,2},{7,3},{8,12},{9,13},{10,... | collective-permute-start | bytes 221192 | tf_op jit(solution)/shard_map/ppermute | solution.py:687
  128.2 14.9 %collective-permute-start.14 = (f32[144,128]{1,0:T(8,128)S(1)}, f32[144,128]{1,0:T(8,128)S(1)}, u32[]{:S(2)}, u32[]{:S(2)}) collective-permute-start(f32[144,128]{1,0:T(8,128)S(1)} %add.136), channel_id=1, source_target_pairs={{0,2},{1,3},{2,4},{3,5},{4,6},{5,7},{6,0},{7,1},{8,10},{9,11},{10,... | collective-permute-start | bytes 221192 | tf_op jit(solution)/shard_map/ppermute | solution.py:687
  129.4 13.6 %collective-permute-start.15 = (f32[144,128]{1,0:T(8,128)S(1)}, f32[144,128]{1,0:T(8,128)S(1)}, u32[]{:S(2)}, u32[]{:S(2)}) collective-permute-start(f32[144,128]{1,0:T(8,128)S(1)} %add.136), channel_id=1, source_target_pairs={{0,6},{1,7},{2,0},{3,1},{4,2},{5,3},{6,4},{7,5},{8,14},{9,15},{10,... | collective-permute-start | bytes 221192 | tf_op jit(solution)/shard_map/ppermute | solution.py:687
  131.5 1.9 copy-start.10
  140.2 2.2 copy-start.14
  142.4 0.7 copy-start.21
  143.1 0.8 copy-start.7
  143.9 0.9 copy-start.4
  144.8 23.9 %collective-permute-start.18 = (f32[144,128]{1,0:T(8,128)S(1)}, f32[144,128]{1,0:T(8,128)S(1)}, u32[]{:S(2)}, u32[]{:S(2)}) collective-permute-start(f32[144,128]{1,0:T(8,128)S(1)} %add_add_fusion.1), channel_id=1, source_target_pairs={{0,16},{1,17},{2,18},{3,19},{4,20},{5,21},{6,22},{7,23},{8,24},{9,... | collective-permute-start | bytes 221192 | tf_op jit(solution)/shard_map/ppermute | solution.py:687
  144.9 23.8 %collective-permute-start.19 = (f32[144,128]{1,0:T(8,128)S(1)}, f32[144,128]{1,0:T(8,128)}, u32[]{:S(2)}, u32[]{:S(2)}) collective-permute-start(f32[144,128]{1,0:T(8,128)S(1)} %add_add_fusion.1), channel_id=1, source_target_pairs={{0,8},{1,9},{2,10},{3,11},{4,12},{5,13},{6,14},{7,15},{8,16},{9,17... | collective-permute-start | bytes 221192 | tf_op jit(solution)/shard_map/ppermute | solution.py:687
  146.9 21.8 %collective-permute-start.20 = (f32[144,128]{1,0:T(8,128)S(1)}, f32[144,128]{1,0:T(8,128)}, u32[]{:S(2)}, u32[]{:S(2)}) collective-permute-start(f32[144,128]{1,0:T(8,128)S(1)} %add_add_fusion.1), channel_id=1, source_target_pairs={{0,24},{1,25},{2,26},{3,27},{4,28},{5,29},{6,30},{7,31},{8,0},{9,1... | collective-permute-start | bytes 221192 | tf_op jit(solution)/shard_map/ppermute | solution.py:687
  148.2 49.8 %all-to-all-start.1 = ((f32[8,768,128]{2,1,0:T(8,128)}), f32[8,768,128]{2,1,0:T(8,128)S(1)}, u32[]{:S(2)}, u32[]{:S(2)}) async-start(f32[8,768,128]{2,1,0:T(8,128)} %get-tuple-element.76.here.above), calls=%async_computation.1 | async-start | bytes 6291456 | tf_op jit(solution)/shard_map/all_to_all | solution.py:691
  152.1 1.1 copy-start.5
  153.2 1.0 copy-start.8
  154.2 1.9 copy-start.11
  156.1 1.0 copy-start.20
  157.1 0.9 copy-start.22
  168.7 4.3 %copy-start.17 = (bf16[8,1152,512]{2,1,0:T(8,128)(2,1)}, bf16[8,1152,512]{2,1,0:T(8,128)(2,1)S(1)}, u32[]{:S(2)}) copy-start(bf16[8,1152,512]{2,1,0:T(8,128)(2,1)S(1)} %get-tuple-element.85.ryz) | copy-start | bytes 28311556
  169.8 4.1 %copy-start.12 = (f32[8,768,128]{2,1,0:T(8,128)S(1)}, f32[8,768,128]{2,1,0:T(8,128)}, u32[]{:S(2)}) copy-start(f32[8,768,128]{2,1,0:T(8,128)} %copy-done.9) | copy-start | bytes 9437188
  169.9 5.5 %copy-start.15 = (bf16[8,1152,256]{2,1,0:T(8,128)(2,1)S(1)}, bf16[8,1152,256]{2,1,0:T(8,128)(2,1)}, u32[]{:S(2)}) copy-start(bf16[8,1152,256]{2,1,0:T(8,128)(2,1)} %copy-done.14) | copy-start | bytes 14155780
  194.4 2.4 collective-permute-start.21
  197.9 27.2 %all-to-all-start.2 = ((f32[16,4,3200]{2,1,0:T(4,128)}), f32[16,4,3200]{2,1,0:T(4,128)}, u32[]{:S(2)}, u32[]{:S(2)}) async-start(f32[16,4,3200]{2,1,0:T(4,128)} %add.159), calls=%async_computation.2 | async-start | bytes 1638400 | tf_op jit(solution)/shard_map/all_to_all | solution.py:691
  204.3 1.9 copy-start.13
  206.2 2.3 copy-start.16
  208.5 18.6 %copy-start.24 = (s32[3]{0:T(128)S(1)}, s32[3]{0:T(128)}, u32[]{:S(2)}) copy-start(s32[3]{0:T(128)} %param.7) | copy-start | bytes 40
  223.5 0.8 copy-start.1
  224.3 0.8 copy-start.6
  227.1 2.4 collective-permute-start.22
  231.8 20.5 %all-to-all-start.3 = ((f32[16,4,2560]{2,1,0:T(4,128)}), f32[16,4,2560]{2,1,0:T(4,128)}, u32[]{:S(2)}, u32[]{:S(2)}) async-start(f32[16,4,2560]{2,1,0:T(4,128)} %add.160), calls=%async_computation.3 | async-start | bytes 1310720 | tf_op jit(solution)/shard_map/all_to_all | solution.py:691

commit v2 on v1

--- a/solution.py
+++ b/solution.py
@@ -339,7 +339,7 @@
         out_specs=(pl.BlockSpec((144, 128), lambda z: (0, 0)), pl.BlockSpec((GRAM, 768, 128), lambda z: (z, 0, 0))),
         out_shape=(jax.ShapeDtypeStruct((144, 128), F32), jax.ShapeDtypeStruct((8, 768, 128), F32)),
         scratch_shapes=[pltpu.VMEM((256, 256), F32)],
-        compiler_params=params(28),
+        compiler_params=params(56),
         cost_estimate=pl.CostEstimate(flops=4_000_000_000, bytes_accessed=3_000_000, transcendentals=0),
         name="gram",
     )(u, first_norm, second_norm)
@@ -406,7 +406,7 @@
             pltpu.VMEM((1, 6, 128, 128), F32),
             pltpu.VMEM((256, 256), F32),
         ],
-        compiler_params=params(20),
+        compiler_params=params(56),
         cost_estimate=pl.CostEstimate(flops=7_000_000_000, bytes_accessed=8_000_000, transcendentals=0),
         name="carry_x",
     )(u, turned, links)
@@ -472,7 +472,7 @@
         out_specs=(pl.BlockSpec((CARRY_YZ, 1152, 512), lambda z: (z, 0, 0)), pl.BlockSpec((128, 128), lambda z: (0, 0))),
         out_shape=(jax.ShapeDtypeStruct((8, 1152, 512), BF16), jax.ShapeDtypeStruct((128, 128), F32)),
         scratch_shapes=[pltpu.VMEM((2, 6, 128, 128), F32), pltpu.VMEM((256, 256), F32)],
-        compiler_params=params(24),
+        compiler_params=params(56),
         cost_estimate=pl.CostEstimate(flops=12_000_000_000, bytes_accessed=16_000_000, transcendentals=0),
         name="carry_yz",
     )(u, turned, u, links, z_up, y_up, x_hops, packed_gram)
@@ -562,7 +562,7 @@
             pltpu.VMEM((count * 256, 2304), BF16),
             pltpu.VMEM((count * 256, 768), F32),
         ],
-        compiler_params=params(40),
+        compiler_params=params(56),
         cost_estimate=pl.CostEstimate(flops=5_500_000_000 * count, bytes_accessed=16_000_000, transcendentals=0),
         name=name,
     )(core, z, turned_u, right_x, right_yz, phases, *([] if extra is None else [extra]))

time: 259 us -> 247 us (0.954)
  local copies, waits for them, and re-layouts: 31.6 us -> 9.59 us
  Pallas kernels: 111 us -> 121 us
    unnamed x52 -> x28, local copies, waits for them, and re-layouts: 29.4 us -> 6.73 us
    pallas_call x2, Pallas kernels: 34 us -> 38.9 us  [elementals(): pl.pallas_call(kernel, grid=(4,), in_specs=[pl.BlockSpec(memory_space=plt...]
  transfers between devices with their start and end apart: 27 -> 27, of which waited for: 4 -> 4; matrix products, arithmetic and copies ran while one was open for 2% -> 2% of each run, Pallas kernels for 38% -> 44%
where the time goes in v2:
time: 247 us; the launch traced here: 246 us
  Pallas kernels  121 us (49%)
  waiting for transfers between devices  55.5 us (22%)
  starting transfers between devices  48.8 us (20%)
  local copies, waits for them, and re-layouts  9.59 us (4%)
  other arithmetic  9.51 us (4%)
    all_to_all x4, waiting for transfers between devices, trade(): lax.all_to_all(value, 'sa', 0, 0, axis_index_groups=groups, tiled=True)  51.4 us
    pallas_call x2, Pallas kernels, elementals(): pl.pallas_call(kernel, grid=(4,), in_specs=[pl.BlockSpec(memory_space=plt...  38.9 us
    pallas_call x3, Pallas kernels, interior(): pl.pallas_call(kernel, grid=(8 // STEP,), in_specs=in_specs, out_specs=ou...  38.5 us
    ppermute x23, starting transfers between devices, move(): return lax.ppermute(value, 'sa', pairs)  27.2 us
    all_to_all x4, starting transfers between devices, trade(): lax.all_to_all(value, 'sa', 0, 0, axis_index_groups=groups, tiled=True)  21.6 us
    pallas_call x1, Pallas kernels, carry_yz(): pl.pallas_call(kernel, grid=(8 // CARRY_YZ,), in_specs=[pl.BlockSpec((CAR...  13 us
    pallas_call x3, Pallas kernels, boundary(): pl.pallas_call(kernel, grid=(8 // FACE,), in_specs=[block, pl.BlockSpec((...  9.73 us
    pallas_call x1, Pallas kernels, carry_x(): pl.pallas_call(kernel, grid=(8 // CARRY_X,), in_specs=[block, block, pl.B...  8.61 us
  transfers between devices with their start and end apart: 27, of which 4 were waited for; matrix products, arithmetic and copies ran while one was open for 2% of the time, Pallas kernels for 44%

profile of v2, /device:TPU:0, one launch (start us, length us, event | category | flops | bytes accessed | tf_op | source)
XLA Modules:
  0.0 246.3 jit_solution(2454641773010782524)
XLA Ops:
  0.6 1.9 copy-done.3
  2.5 1.2 copy-done.4
  3.7 1.5 lay_out.1
  5.2 1.7 copy-done
  6.9 4.7 %all-to-all-start = ((f32[8,840,128]{2,1,0:T(8,128)}), f32[8,840,128]{2,1,0:T(8,128)S(1)}, u32[]{:S(2)}, u32[]{:S(2)}) async-start(f32[8,840,128]{2,1,0:T(8,128)} %copy-done), calls=%async_computation | async-start | bytes 6881280 | tf_op jit(solution)/shard_map/all_to_all | solution.py:691
  11.9 0.1 add.152
  11.9 0.1 fusion.18
  12.0 0.2 fusion.11
  12.2 41.0 %all-to-all-done.refs_0_.refs_1_.refs_3_ = f32[8,840,128]{2,1,0:T(8,128)S(1)} async-done(((f32[8,840,128]{2,1,0:T(8,128)}), f32[8,840,128]{2,1,0:T(8,128)S(1)}, u32[]{:S(2)}, u32[]{:S(2)}) %all-to-all-start) | async-done | bytes 3440672 | tf_op jit(solution)/shard_map/all_to_all | solution.py:691
  53.2 2.0 collective-permute-start.1
  55.2 0.2 slice.79
  55.4 0.2 fusion.26
  55.6 0.1 collective-permute-start.2
  55.7 0.4 collective-permute-start.3
  56.1 2.2 collective-permute-start
  58.3 12.9 %interior_0.1 = (f32[8,768,128]{2,1,0:T(8,128)S(1)}, f32[8,128]{1,0:T(8,128)}, f32[8,128,128]{2,1,0:T(8,128)S(1)}) custom-call(f32[8,840,128]{2,1,0:T(8,128)S(1)} %all-to-all-done.refs_0_.refs_1_.refs_3_, f32[8,840,128]{2,1,0:T(8,128)S(1)} %all-to-all-done.refs_0_.refs_1_.refs_3_), custom_call_target="tpu_custom_call" | custom-call | flops 12000000000 | bytes 12000000 | tf_op jit(solution)/shard_map/interior_0/pallas_call | solution.py:188
  71.3 2.8 %boundary_0.1 = (f32[8,768,128]{2,1,0:T(8,128)S(1)}, f32[8,6,32,128]{3,2,1,0:T(8,128)S(1)}, f32[8,6,32,128]{3,2,1,0:T(8,128)S(1)}, f32[768,128]{1,0:T(8,128)S(1)}, f32[768,128]{1,0:T(8,128)S(1)}) custom-call(f32[8,768,128]{2,1,0:T(8,128)S(1)} %get-tuple-element.51.part, f32[8,128,128]{2,1,0:T(8,128)S(1)} %get-tuple-element.52.link_ref.refs_2_, ...), custom_call_target="tpu_custom_call" | custom-call | flops 6000000000 | bytes 9000000 | tf_op jit(solution)/shard_map/boundary_0/pallas_call | solution.py:263
  74.1 2.6 %collective-permute-start.6 = (f32[8,6,32,128]{3,2,1,0:T(8,128)S(1)}, f32[8,6,32,128]{3,2,1,0:T(8,128)S(1)}, u32[]{:S(2)}, u32[]{:S(2)}) collective-permute-start(f32[8,6,32,128]{3,2,1,0:T(8,128)S(1)} %get-tuple-element.57), channel_id=1, source_target_pairs={{0,7},{1,0},{2,1},{3,2},{4,3},{5,4},{6,5},{7,6},{8,15},{9,8},{10,9... | collective-permute-start | bytes 2359304 | tf_op jit(solution)/shard_map/ppermute | solution.py:687
  76.7 1.7 collective-permute-start.4
  78.4 0.3 collective-permute-start.5
  78.7 12.9 %interior_1.1 = (f32[8,768,128]{2,1,0:T(8,128)S(1)}, f32[8,128]{1,0:T(8,128)S(1)}) custom-call(f32[8,768,128]{2,1,0:T(8,128)S(1)} %get-tuple-element.53.refs_0_.refs_1_.refs_3_, f32[8,768,128]{2,1,0:T(8,128)S(1)} %get-tuple-element.53.refs_0_.refs_1_.refs_3_, f32[8,128,128]{2,1,0:T(8,128)S(1)} %get-tuple-element.52.link_ref.refs_2_, ...), custom_call_target="tpu_custom_call" | custom-call | flops 12000000000 | bytes 12000000 | tf_op jit(solution)/shard_map/interior_1/pallas_call | solution.py:188
  91.7 2.8 %boundary_1.1 = (f32[8,768,128]{2,1,0:T(8,128)S(1)}, f32[8,6,32,128]{3,2,1,0:T(8,128)S(1)}, f32[8,6,32,128]{3,2,1,0:T(8,128)S(1)}, f32[768,128]{1,0:T(8,128)S(1)}, f32[768,128]{1,0:T(8,128)S(1)}) custom-call(f32[8,768,128]{2,1,0:T(8,128)S(1)} %get-tuple-element.54.part, f32[8,128,128]{2,1,0:T(8,128)S(1)} %get-tuple-element.52.link_ref.refs_2_, ...), custom_call_target="tpu_custom_call" | custom-call | flops 6000000000 | bytes 9000000 | tf_op jit(solution)/shard_map/boundary_1/pallas_call | solution.py:263
  94.5 2.4 collective-permute-start.10
  96.9 2.9 %collective-permute-start.8 = (f32[768,128]{1,0:T(8,128)S(1)}, f32[768,128]{1,0:T(8,128)S(1)}, u32[]{:S(2)}, u32[]{:S(2)}) collective-permute-start(f32[768,128]{1,0:T(8,128)S(1)} %get-tuple-element.61), channel_id=1, source_target_pairs={{0,24},{1,25},{2,26},{3,27},{4,28},{5,29},{6,30},{7,31},{8,0},{9,1... | collective-permute-start | bytes 1179656 | tf_op jit(solution)/shard_map/ppermute | solution.py:687
  99.8 12.7 %interior_2.1 = (f32[8,768,128]{2,1,0:T(8,128)S(1)}, f32[8,128]{1,0:T(8,128)S(1)}) custom-call(f32[8,768,128]{2,1,0:T(8,128)S(1)} %get-tuple-element.59.refs_0_.refs_1_, f32[8,768,128]{2,1,0:T(8,128)S(1)} %get-tuple-element.59.refs_0_.refs_1_, f32[8,128,128]{2,1,0:T(8,128)S(1)} %get-tuple-element.52.link_ref.refs_2_, ...), custom_call_target="tpu_custom_call" | custom-call | flops 12000000000 | bytes 12000000 | tf_op jit(solution)/shard_map/interior_2/pallas_call | solution.py:188
  112.6 4.2 %boundary_2.1 = (f32[8,768,128]{2,1,0:T(8,128)}, f32[8,6,32,128]{3,2,1,0:T(8,128)S(1)}, f32[8,6,32,128]{3,2,1,0:T(8,128)}, f32[768,128]{1,0:T(8,128)S(1)}, f32[768,128]{1,0:T(8,128)}) custom-call(f32[8,768,128]{2,1,0:T(8,128)S(1)} %get-tuple-element.60.part, f32[8,128,128]{2,1,0:T(8,128)S(1)} %get-tuple-element.52.link_ref.refs_2_, ...), custom_call_target="tpu_custom_call" | custom-call | flops 6000000000 | bytes 9000000 | tf_op jit(solution)/shard_map/boundary_2/pallas_call | solution.py:263
  116.7 2.7 %collective-permute-start.17 = (f32[8,6,32,128]{3,2,1,0:T(8,128)S(1)}, f32[8,6,32,128]{3,2,1,0:T(8,128)S(1)}, u32[]{:S(2)}, u32[]{:S(2)}) collective-permute-start(f32[8,6,32,128]{3,2,1,0:T(8,128)S(1)} %get-tuple-element.72), channel_id=1, source_target_pairs={{0,7},{1,0},{2,1},{3,2},{4,3},{5,4},{6,5},{7,6},{8,15},{9,8},{10,9... | collective-permute-start | bytes 2359304 | tf_op jit(solution)/shard_map/ppermute | solution.py:687
  119.4 4.7 %gram.1 = (f32[144,128]{1,0:T(8,128)}, f32[8,768,128]{2,1,0:T(8,128)}) custom-call(f32[8,768,128]{2,1,0:T(8,128)} %get-tuple-element.76.here.above, f32[8,128]{1,0:T(8,128)} %copy-done.6, f32[8,128]{1,0:T(8,128)} %copy-done.7), custom_call_target="tpu_custom_call" | custom-call | flops 4000000000 | bytes 3000000 | tf_op jit(solution)/shard_map/gram/pallas_call | solution.py:335
  124.1 0.6 copy.20
  124.7 3.0 %collective-permute-start.16 = (f32[768,128]{1,0:T(8,128)S(1)}, f32[768,128]{1,0:T(8,128)S(1)}, u32[]{:S(2)}, u32[]{:S(2)}) collective-permute-start(f32[768,128]{1,0:T(8,128)S(1)} %get-tuple-element.71), channel_id=1, source_target_pairs={{0,24},{1,25},{2,26},{3,27},{4,28},{5,29},{6,30},{7,31},{8,0},{9,1... | collective-permute-start | bytes 1179656 | tf_op jit(solution)/shard_map/ppermute | solution.py:687
  127.7 0.9 add.136
  128.6 0.1 collective-permute-start.13
  128.7 1.3 collective-permute-start.14
  129.9 2.0 collective-permute-start.15
  132.0 8.6 %carry_x.1 = (bf16[8,1152,256]{2,1,0:T(8,128)(2,1)}, f32[256,256]{1,0:T(8,128)}) custom-call(f32[8,768,128]{2,1,0:T(8,128)} %get-tuple-element.76.here.above, f32[8,768,128]{2,1,0:T(8,128)} %get-tuple-element.90.turned.here, f32[8,128,128]{2,1,0:T(8,128)} %copy-done.5), custom_call_target="tpu_custom_call" | custom-call | flops 7000000000 | bytes 8000000 | tf_op jit(solution)/shard_map/carry_x/pallas_call | solution.py:398
  140.7 0.1 collective-permute-start.18
  140.8 0.6 copy-done.11
  141.4 1.1 collective-permute-start.19
  142.5 2.2 collective-permute-start.20
  144.6 3.9 %all-to-all-start.1 = ((f32[8,768,128]{2,1,0:T(8,128)}), f32[8,768,128]{2,1,0:T(8,128)S(1)}, u32[]{:S(2)}, u32[]{:S(2)}) async-start(f32[8,768,128]{2,1,0:T(8,128)} %get-tuple-element.76.here.above), calls=%async_computation.1 | async-start | bytes 6291456 | tf_op jit(solution)/shard_map/all_to_all | solution.py:691
  148.5 13.0 %carry_yz.1 = (bf16[8,1152,512]{2,1,0:T(8,128)(2,1)}, f32[128,128]{1,0:T(8,128)}) custom-call(f32[8,768,128]{2,1,0:T(8,128)} %get-tuple-element.76.here.above, f32[8,768,128]{2,1,0:T(8,128)} %get-tuple-element.90.turned.here, f32[8,768,128]{2,1,0:T(8,128)} %get-tuple-element.76.here.above, f32[8,128,128]{2,1,0:T(8,128)} %copy-done.5, f32[768,128]{1,0:T(8,128)} %copy-done.11, ...), custom_call_target="tpu_custom_call" | custom-call | flops 12000000000 | bytes 16000000 | tf_op jit(solution)/shard_map/carry_yz/pallas_call | solution.py:459
  161.6 1.6 newton.1.z_ref
  163.2 0.6 copy-done.1
  163.9 21.2 %elementals_0.1 = (f32[16,4,3200]{2,1,0:T(4,128)}, f32[16,4,3200]{2,1,0:T(4,128)}) custom-call(s32[1]{0:T(128)} %bitcast.5.core_ref, f32[2,128,128]{2,1,0:T(8,128)} %copy-done.1, f32[8,768,128]{2,1,0:T(8,128)} %get-tuple-element.90.turned.here, bf16[8,1152,256]{2,1,0:T(8,128)(2,1)} %get-tuple-element.84.rx, bf16[8,1152,512]{2,1,0:T(8,128)(2,1)} %get-tuple-element.85.ryz, ...), custom_call_target="tpu_custom_call" | custom-call | flops 22000001024 | bytes 16000000 | tf_op jit(solution)/shard_map/elementals_0/pallas_call | solution.py:547
  185.1 0.2 collective-permute-start.21
  185.2 2.4 collective-permute-done.21
  187.6 2.3 add.159
  189.9 5.8 %all-to-all-start.2 = ((f32[16,4,3200]{2,1,0:T(4,128)}), f32[16,4,3200]{2,1,0:T(4,128)}, u32[]{:S(2)}, u32[]{:S(2)}) async-start(f32[16,4,3200]{2,1,0:T(4,128)} %add.159), calls=%async_computation.2 | async-start | bytes 1638400 | tf_op jit(solution)/shard_map/all_to_all | solution.py:691
  195.7 17.7 %elementals_1.1 = (f32[16,4,2560]{2,1,0:T(4,128)}, f32[16,4,2560]{2,1,0:T(4,128)}) custom-call(s32[1]{0:T(128)} %bitcast.5.core_ref, f32[2,128,128]{2,1,0:T(8,128)} %copy-done.1, f32[8,768,128]{2,1,0:T(8,128)} %get-tuple-element.90.turned.here, bf16[8,1152,256]{2,1,0:T(8,128)(2,1)} %get-tuple-element.84.rx, bf16[8,1152,512]{2,1,0:T(8,128)(2,1)} %get-tuple-element.85.ryz, ...), custom_call_target="tpu_custom_call" | custom-call | flops 16499999744 | bytes 16000000 | tf_op jit(solution)/shard_map/elementals_1/pallas_call | solution.py:547
  213.4 1.3 reduce_sum.27
  214.7 0.6 broadcast_dynamic-update-slice_fusion
  215.4 0.7 slice_bitcast_fusion.2
  216.1 1.7 collective-permute-done.22
  217.8 2.3 add.160
  220.1 7.2 %all-to-all-start.3 = ((f32[16,4,2560]{2,1,0:T(4,128)}), f32[16,4,2560]{2,1,0:T(4,128)}, u32[]{:S(2)}, u32[]{:S(2)}) async-start(f32[16,4,2560]{2,1,0:T(4,128)} %add.160), calls=%async_computation.3 | async-start | bytes 1310720 | tf_op jit(solution)/shard_map/all_to_all | solution.py:691
  227.4 2.7 %rotate.1 = f32[6,1024,128]{2,1,0:T(8,128)} custom-call(f32[2,128,128]{2,1,0:T(8,128)S(1)} %copy-done.2, f32[8,768,128]{2,1,0:T(8,128)S(1)} %all-to-all-done.1.ref), custom_call_target="tpu_custom_call" | custom-call | flops 5000000000 | bytes 7000000 | tf_op jit(solution)/shard_map/rotate/pallas_call | solution.py:654
  230.2 10.4 %all-to-all-done.3 = f32[16,4,2560]{2,1,0:T(4,128)} async-done(((f32[16,4,2560]{2,1,0:T(4,128)}), f32[16,4,2560]{2,1,0:T(4,128)}, u32[]{:S(2)}, u32[]{:S(2)}) %all-to-all-start.3) | async-done | bytes 655392 | tf_op jit(solution)/shard_map/all_to_all | solution.py:691
  240.6 1.1 slice_reduce_fusion
  241.8 0.2 slice_reduce_fusion.2
  242.1 1.2 convolution_multiply_fusion
  243.3 0.1 select_reduce_fusion
  243.5 0.7 copy.16
  244.2 0.8 select_bitcast_fusion.1
  245.0 1.3 rayleigh.1
  (75 shorter events, 0.8 us)
Async XLA Ops:
  0.6 1.9 copy-start.3
  2.5 1.2 copy-start.4
  5.2 1.7 copy-start
  6.9 4.7 %copy-start.9 = (s32[7,3]{0,1:T(4,128)S(1)}, s32[7,3]{0,1:T(4,128)}, u32[]{:S(2)}) copy-start(s32[7,3]{0,1:T(4,128)} %param.6) | copy-start | bytes 256
  6.9 46.3 %all-to-all-start = ((f32[8,840,128]{2,1,0:T(8,128)}), f32[8,840,128]{2,1,0:T(8,128)S(1)}, u32[]{:S(2)}, u32[]{:S(2)}) async-start(f32[8,840,128]{2,1,0:T(8,128)} %copy-done), calls=%async_computation | async-start | bytes 6881280 | tf_op jit(solution)/shard_map/all_to_all | solution.py:691
  53.2 18.0 %collective-permute-start.1 = (f32[840,128]{1,0:T(8,128)S(1)}, f32[840,128]{1,0:T(8,128)S(1)}, u32[]{:S(2)}, u32[]{:S(2)}) collective-permute-start(f32[840,128]{1,0:T(8,128)S(1)} %slice_bitcast_fusion), channel_id=1, source_target_pairs={{0,8},{1,9},{2,10},{3,11},{4,12},{5,13},{6,14},{7,15},{8,16},{9,17... | collective-permute-start | bytes 1290248 | tf_op jit(solution)/shard_map/ppermute | solution.py:687
  55.6 15.7 %collective-permute-start.2 = (f32[8,6,32,128]{3,2,1,0:T(8,128)S(1)}, f32[8,6,32,128]{3,2,1,0:T(8,128)S(1)}, u32[]{:S(2)}, u32[]{:S(2)}) collective-permute-start(f32[8,6,32,128]{3,2,1,0:T(8,128)S(1)} %get-tuple-element.111), channel_id=1, source_target_pairs={{0,7},{1,0},{2,1},{3,2},{4,3},{5,4},{6,5},{7,6},{8,15},{9,8},{10,9... | collective-permute-start | bytes 2359304 | tf_op jit(solution)/shard_map/ppermute | solution.py:687
  55.7 15.6 %collective-permute-start.3 = (f32[8,6,32,128]{3,2,1,0:T(8,128)S(1)}, f32[8,6,32,128]{3,2,1,0:T(8,128)S(1)}, u32[]{:S(2)}, u32[]{:S(2)}) collective-permute-start(f32[8,6,32,128]{3,2,1,0:T(8,128)S(1)} %get-tuple-element.110), channel_id=1, source_target_pairs={{0,1},{1,2},{2,3},{3,4},{4,5},{5,6},{6,7},{7,0},{8,9},{9,10},{10,1... | collective-permute-start | bytes 2359304 | tf_op jit(solution)/shard_map/ppermute | solution.py:687
  56.1 15.2 %collective-permute-start = (f32[768,128]{1,0:T(8,128)S(1)}, f32[768,128]{1,0:T(8,128)S(1)}, u32[]{:S(2)}, u32[]{:S(2)}) collective-permute-start(f32[768,128]{1,0:T(8,128)S(1)} %slice_bitcast_fusion.1), channel_id=1, source_target_pairs={{0,24},{1,25},{2,26},{3,27},{4,28},{5,29},{6,30},{7,31},{8,0},{9,1... | collective-permute-start | bytes 1179656 | tf_op jit(solution)/shard_map/ppermute | solution.py:687
  71.3 41.3 %copy-start.5 = (f32[8,128,128]{2,1,0:T(8,128)}, f32[8,128,128]{2,1,0:T(8,128)S(1)}, u32[]{:S(2)}) copy-start(f32[8,128,128]{2,1,0:T(8,128)S(1)} %get-tuple-element.52.link_ref.refs_2_) | copy-start | bytes 1572868
  74.1 17.5 %collective-permute-start.6 = (f32[8,6,32,128]{3,2,1,0:T(8,128)S(1)}, f32[8,6,32,128]{3,2,1,0:T(8,128)S(1)}, u32[]{:S(2)}, u32[]{:S(2)}) collective-permute-start(f32[8,6,32,128]{3,2,1,0:T(8,128)S(1)} %get-tuple-element.57), channel_id=1, source_target_pairs={{0,7},{1,0},{2,1},{3,2},{4,3},{5,4},{6,5},{7,6},{8,15},{9,8},{10,9... | collective-permute-start | bytes 2359304 | tf_op jit(solution)/shard_map/ppermute | solution.py:687
  76.7 15.0 %collective-permute-start.7 = (f32[8,6,32,128]{3,2,1,0:T(8,128)S(1)}, f32[8,6,32,128]{3,2,1,0:T(8,128)S(1)}, u32[]{:S(2)}, u32[]{:S(2)}) collective-permute-start(f32[8,6,32,128]{3,2,1,0:T(8,128)S(1)} %get-tuple-element.58), channel_id=1, source_target_pairs={{0,1},{1,2},{2,3},{3,4},{4,5},{5,6},{6,7},{7,0},{8,9},{9,10},{10,1... | collective-permute-start | bytes 2359304 | tf_op jit(solution)/shard_map/ppermute | solution.py:687
  76.7 14.9 %collective-permute-start.4 = (f32[768,128]{1,0:T(8,128)S(1)}, f32[768,128]{1,0:T(8,128)S(1)}, u32[]{:S(2)}, u32[]{:S(2)}) collective-permute-start(f32[768,128]{1,0:T(8,128)S(1)} %get-tuple-element.55), channel_id=1, source_target_pairs={{0,24},{1,25},{2,26},{3,27},{4,28},{5,29},{6,30},{7,31},{8,0},{9,1... | collective-permute-start | bytes 1179656 | tf_op jit(solution)/shard_map/ppermute | solution.py:687
  78.4 13.2 %collective-permute-start.5 = (f32[768,128]{1,0:T(8,128)S(1)}, f32[768,128]{1,0:T(8,128)S(1)}, u32[]{:S(2)}, u32[]{:S(2)}) collective-permute-start(f32[768,128]{1,0:T(8,128)S(1)} %get-tuple-element.56), channel_id=1, source_target_pairs={{0,8},{1,9},{2,10},{3,11},{4,12},{5,13},{6,14},{7,15},{8,16},{9,17... | collective-permute-start | bytes 1179656 | tf_op jit(solution)/shard_map/ppermute | solution.py:687
  91.6 2.9 %copy-start.6 = (f32[8,128]{1,0:T(8,128)}, f32[8,128]{1,0:T(8,128)S(1)}, u32[]{:S(2)}) copy-start(f32[8,128]{1,0:T(8,128)S(1)} %get-tuple-element.66.n1) | copy-start | bytes 12292
  94.5 18.1 %collective-permute-start.10 = (f32[8,6,32,128]{3,2,1,0:T(8,128)S(1)}, f32[8,6,32,128]{3,2,1,0:T(8,128)S(1)}, u32[]{:S(2)}, u32[]{:S(2)}) collective-permute-start(f32[8,6,32,128]{3,2,1,0:T(8,128)S(1)} %get-tuple-element.63), channel_id=1, source_target_pairs={{0,7},{1,0},{2,1},{3,2},{4,3},{5,4},{6,5},{7,6},{8,15},{9,8},{10,9... | collective-permute-start | bytes 2359304 | tf_op jit(solution)/shard_map/ppermute | solution.py:687
  96.9 15.7 %collective-permute-start.11 = (f32[8,6,32,128]{3,2,1,0:T(8,128)S(1)}, f32[8,6,32,128]{3,2,1,0:T(8,128)S(1)}, u32[]{:S(2)}, u32[]{:S(2)}) collective-permute-start(f32[8,6,32,128]{3,2,1,0:T(8,128)S(1)} %get-tuple-element.64), channel_id=1, source_target_pairs={{0,1},{1,2},{2,3},{3,4},{4,5},{5,6},{6,7},{7,0},{8,9},{9,10},{10,1... | collective-permute-start | bytes 2359304 | tf_op jit(solution)/shard_map/ppermute | solution.py:687
  96.9 15.6 %collective-permute-start.8 = (f32[768,128]{1,0:T(8,128)S(1)}, f32[768,128]{1,0:T(8,128)S(1)}, u32[]{:S(2)}, u32[]{:S(2)}) collective-permute-start(f32[768,128]{1,0:T(8,128)S(1)} %get-tuple-element.61), channel_id=1, source_target_pairs={{0,24},{1,25},{2,26},{3,27},{4,28},{5,29},{6,30},{7,31},{8,0},{9,1... | collective-permute-start | bytes 1179656 | tf_op jit(solution)/shard_map/ppermute | solution.py:687
  99.8 12.7 %collective-permute-start.9 = (f32[768,128]{1,0:T(8,128)S(1)}, f32[768,128]{1,0:T(8,128)S(1)}, u32[]{:S(2)}, u32[]{:S(2)}) collective-permute-start(f32[768,128]{1,0:T(8,128)S(1)} %get-tuple-element.62), channel_id=1, source_target_pairs={{0,8},{1,9},{2,10},{3,11},{4,12},{5,13},{6,14},{7,15},{8,16},{9,17... | collective-permute-start | bytes 1179656 | tf_op jit(solution)/shard_map/ppermute | solution.py:687
  112.5 4.2 %copy-start.7 = (f32[8,128]{1,0:T(8,128)}, f32[8,128]{1,0:T(8,128)S(1)}, u32[]{:S(2)}) copy-start(f32[8,128]{1,0:T(8,128)S(1)} %get-tuple-element.67.n2) | copy-start | bytes 12292
  116.7 23.9 %collective-permute-start.17 = (f32[8,6,32,128]{3,2,1,0:T(8,128)S(1)}, f32[8,6,32,128]{3,2,1,0:T(8,128)S(1)}, u32[]{:S(2)}, u32[]{:S(2)}) collective-permute-start(f32[8,6,32,128]{3,2,1,0:T(8,128)S(1)} %get-tuple-element.72), channel_id=1, source_target_pairs={{0,7},{1,0},{2,1},{3,2},{4,3},{5,4},{6,5},{7,6},{8,15},{9,8},{10,9... | collective-permute-start | bytes 2359304 | tf_op jit(solution)/shard_map/ppermute | solution.py:687
  124.1 3.6 %collective-permute-start.12 = (f32[144,128]{1,0:T(8,128)}, f32[144,128]{1,0:T(8,128)S(1)}, u32[]{:S(2)}, u32[]{:S(2)}) collective-permute-start(f32[144,128]{1,0:T(8,128)} %get-tuple-element.68.gram_ref), channel_id=1, source_target_pairs={{0,1},{1,0},{2,3},{3,2},{4,5},{5,4},{6,7},{7,6},{8,9},{9,8},{10,11... | collective-permute-start | bytes 221192 | tf_op jit(solution)/shard_map/ppermute | solution.py:687
  124.7 15.9 %collective-permute-start.16 = (f32[768,128]{1,0:T(8,128)S(1)}, f32[768,128]{1,0:T(8,128)S(1)}, u32[]{:S(2)}, u32[]{:S(2)}) collective-permute-start(f32[768,128]{1,0:T(8,128)S(1)} %get-tuple-element.71), channel_id=1, source_target_pairs={{0,24},{1,25},{2,26},{3,27},{4,28},{5,29},{6,30},{7,31},{8,0},{9,1... | collective-permute-start | bytes 1179656 | tf_op jit(solution)/shard_map/ppermute | solution.py:687
  128.6 12.0 %collective-permute-start.13 = (f32[144,128]{1,0:T(8,128)S(1)}, f32[144,128]{1,0:T(8,128)S(1)}, u32[]{:S(2)}, u32[]{:S(2)}) collective-permute-start(f32[144,128]{1,0:T(8,128)S(1)} %add.136), channel_id=1, source_target_pairs={{0,4},{1,5},{2,6},{3,7},{4,0},{5,1},{6,2},{7,3},{8,12},{9,13},{10,... | collective-permute-start | bytes 221192 | tf_op jit(solution)/shard_map/ppermute | solution.py:687
  128.7 11.9 %collective-permute-start.14 = (f32[144,128]{1,0:T(8,128)S(1)}, f32[144,128]{1,0:T(8,128)S(1)}, u32[]{:S(2)}, u32[]{:S(2)}) collective-permute-start(f32[144,128]{1,0:T(8,128)S(1)} %add.136), channel_id=1, source_target_pairs={{0,2},{1,3},{2,4},{3,5},{4,6},{5,7},{6,0},{7,1},{8,10},{9,11},{10,... | collective-permute-start | bytes 221192 | tf_op jit(solution)/shard_map/ppermute | solution.py:687
  129.9 10.7 %collective-permute-start.15 = (f32[144,128]{1,0:T(8,128)S(1)}, f32[144,128]{1,0:T(8,128)S(1)}, u32[]{:S(2)}, u32[]{:S(2)}) collective-permute-start(f32[144,128]{1,0:T(8,128)S(1)} %add.136), channel_id=1, source_target_pairs={{0,6},{1,7},{2,0},{3,1},{4,2},{5,3},{6,4},{7,5},{8,14},{9,15},{10,... | collective-permute-start | bytes 221192 | tf_op jit(solution)/shard_map/ppermute | solution.py:687
  140.6 0.7 copy-start.11
  140.7 4.0 %copy-start.10 = (f32[8,6,32,128]{3,2,1,0:T(8,128)}, f32[8,6,32,128]{3,2,1,0:T(8,128)S(1)}, u32[]{:S(2)}) copy-start(f32[8,6,32,128]{3,2,1,0:T(8,128)S(1)} %collective-permute-done.17.yu) | copy-start | bytes 2359300
  140.7 20.8 %collective-permute-start.18 = (f32[144,128]{1,0:T(8,128)S(1)}, f32[144,128]{1,0:T(8,128)S(1)}, u32[]{:S(2)}, u32[]{:S(2)}) collective-permute-start(f32[144,128]{1,0:T(8,128)S(1)} %add_add_fusion.1), channel_id=1, source_target_pairs={{0,16},{1,17},{2,18},{3,19},{4,20},{5,21},{6,22},{7,23},{8,24},{9,... | collective-permute-start | bytes 221192 | tf_op jit(solution)/shard_map/ppermute | solution.py:687
  141.4 20.2 %collective-permute-start.19 = (f32[144,128]{1,0:T(8,128)S(1)}, f32[144,128]{1,0:T(8,128)S(1)}, u32[]{:S(2)}, u32[]{:S(2)}) collective-permute-start(f32[144,128]{1,0:T(8,128)S(1)} %add_add_fusion.1), channel_id=1, source_target_pairs={{0,8},{1,9},{2,10},{3,11},{4,12},{5,13},{6,14},{7,15},{8,16},{9,17... | collective-permute-start | bytes 221192 | tf_op jit(solution)/shard_map/ppermute | solution.py:687
  142.5 19.1 %collective-permute-start.20 = (f32[144,128]{1,0:T(8,128)S(1)}, f32[144,128]{1,0:T(8,128)S(1)}, u32[]{:S(2)}, u32[]{:S(2)}) collective-permute-start(f32[144,128]{1,0:T(8,128)S(1)} %add_add_fusion.1), channel_id=1, source_target_pairs={{0,24},{1,25},{2,26},{3,27},{4,28},{5,29},{6,30},{7,31},{8,0},{9,1... | collective-permute-start | bytes 221192 | tf_op jit(solution)/shard_map/ppermute | solution.py:687
  144.6 45.3 %all-to-all-start.1 = ((f32[8,768,128]{2,1,0:T(8,128)}), f32[8,768,128]{2,1,0:T(8,128)S(1)}, u32[]{:S(2)}, u32[]{:S(2)}) async-start(f32[8,768,128]{2,1,0:T(8,128)} %get-tuple-element.76.here.above), calls=%async_computation.1 | async-start | bytes 6291456 | tf_op jit(solution)/shard_map/all_to_all | solution.py:691
  163.2 0.7 copy-start.1
  185.1 2.5 %collective-permute-start.21 = (f32[16,4,3200]{2,1,0:T(4,128)}, f32[16,4,3200]{2,1,0:T(4,128)S(1)}, u32[]{:S(2)}, u32[]{:S(2)}) collective-permute-start(f32[16,4,3200]{2,1,0:T(4,128)} %get-tuple-element.88), channel_id=1, source_target_pairs={{0,1},{1,0},{2,3},{3,2},{4,5},{5,4},{6,7},{7,6},{8,9},{9,8},{10,11... | collective-permute-start | bytes 2457608 | tf_op jit(solution)/shard_map/ppermute | solution.py:687
  189.9 23.5 %all-to-all-start.2 = ((f32[16,4,3200]{2,1,0:T(4,128)}), f32[16,4,3200]{2,1,0:T(4,128)}, u32[]{:S(2)}, u32[]{:S(2)}) async-start(f32[16,4,3200]{2,1,0:T(4,128)} %add.159), calls=%async_computation.2 | async-start | bytes 1638400 | tf_op jit(solution)/shard_map/all_to_all | solution.py:691
  195.7 19.6 %copy-start.12 = (s32[3]{0:T(128)S(1)}, s32[3]{0:T(128)}, u32[]{:S(2)}) copy-start(s32[3]{0:T(128)} %param.7) | copy-start | bytes 40
  195.7 19.7 %copy-start.2 = (f32[2,128,128]{2,1,0:T(8,128)S(1)}, f32[2,128,128]{2,1,0:T(8,128)}, u32[]{:S(2)}) copy-start(f32[2,128,128]{2,1,0:T(8,128)} %copy-done.1) | copy-start | bytes 393220
  215.3 2.4 collective-permute-start.22
  220.1 20.5 %all-to-all-start.3 = ((f32[16,4,2560]{2,1,0:T(4,128)}), f32[16,4,2560]{2,1,0:T(4,128)}, u32[]{:S(2)}, u32[]{:S(2)}) async-start(f32[16,4,2560]{2,1,0:T(4,128)} %add.160), calls=%async_computation.3 | async-start | bytes 1310720 | tf_op jit(solution)/shard_map/all_to_all | solution.py:691
  227.4 14.6 %copy-start.8 = (f32[128,128]{1,0:T(8,128)S(1)}, f32[128,128]{1,0:T(8,128)}, u32[]{:S(2)}) copy-start(f32[128,128]{1,0:T(8,128)} %get-tuple-element.114) | copy-start | bytes 196612
